TPU v7x, 32 devices: a whole 2x2x4 slice. The times are simulated.
32 devices in a mesh: gz: 8 (over z, x), gy: 4 (over y, core).
Axes of the slice: x: 2, y: 2, z: 4, core: 2. Of those that a mesh axis runs over, the one named last changes fastest.
Arguments:
- excess_warmth: float32 [384, 6144], P('gz', 'gy'), may hold values from -6 to 6
- pore_moisture: float32 [384, 6144], P('gz', 'gy'), may hold values from 0.55 to 1
- cement_maturity_degree: float32 [384, 6144], P('gz', 'gy'), may hold values from 0.05 to 0.85
- parcel_filled_tally: int32 [384, 48], P('gz', 'gy'), may hold values from 0 to 128
- parcel_keeper_position: int32 [384, 48], P('gz', 'gy'), may hold values from 0 to 1727, as said below
- layer_pouring_times: int32 [48], replicated, may hold values from 0 to 2000
- voigt_strains_stored: float32 [55296, 8, 128], P(('gz', 'gy')), may hold values from -4 to 4
- micro_tension: float32 [55296, 128], P(('gz', 'gy')), may hold values from 0.5 to 5
Outputs:
- temperature_new: float32 [384, 6144], P('gz', 'gy')
- humidity_new: float32 [384, 6144], P('gz', 'gy')
- cement_maturity_after: float32 [384, 6144], P('gz', 'gy')
- creep_strain: float32 [384, 6144], P('gz', 'gy')
- voigt_strains_after: float32 [55296, 8, 128], P(('gz', 'gy'))
- micro_tension_after: float32 [55296, 128], P(('gz', 'gy'))
Inputs may be any that keep to these rules, and one draw needn't show every extreme that they name: `parcel_keeper_position`: number the devices gz index * 4 + gy index. The 576 blocks on one device carry distinct values; value // 54 is the device that holds the block's creep state. In every draw one device holds the states of exactly 54 blocks of every device.
All inputs are finite; a program needn't handle non-finite values.
Results may differ from a plain program's by a relative error of at most 0.00002.
Values sent between devices are 32-bit elements; how exact they have to be, the bound alone decides.
A program may use at most 64 MiB of HBM per device.

v0:
```python
import jax
import jax.numpy as jnp
from jax import lax
from jax.sharding import PartitionSpec as P

NX = 48
PARCEL_SITES = 128
SWEEPS = 3
LIFT = 8


rate_base = 0.05
activation = 0.5
cement_warmth_output = 4.0
desiccation = 0.5
diff_floor = 0.05
humid_scale = 5.0
expansion_factor = 0.5
drying_contraction_factor = 2.0
now_hours = 2400.0
age_scale = 600.0
creep_activation = 0.3
kelvin_amp = 0.15
micro_rate = 0.2
flow_coef = 0.1


def with_halo(cells, sides, width):
    for axis, dim in sides:
        count = lax.axis_size(axis)
        ends = count - 1
        head = lax.slice_in_dim(cells, 0, width, axis=dim)
        tail = lax.slice_in_dim(cells, cells.shape[dim] - width, cells.shape[dim], axis=dim)
        cells = jnp.concatenate(
            [
                lax.ppermute(tail, axis, [(i, (i + 1) % count) for i in range(ends)]),
                cells,
                lax.ppermute(head, axis, [((i + 1) % count, i) for i in range(ends)]),
            ],
            axis=dim,
        )
    return cells


def cement_maturing_speed(field_temp, field_hum, degree):
    humid_term = 7.5 - 7.5 * field_hum
    humid_term = humid_term * humid_term
    return (
        rate_base
        * (1.0 - degree)
        * jnp.exp(activation * field_temp)
        / (1.0 + humid_term * humid_term)
    )


def diffusivity(field_hum):
    ratio = humid_scale * (1.0 - field_hum)
    power = ratio * ratio
    power = power * power
    power = power * power
    power = power * power
    return diff_floor + (1.0 - diff_floor) / (1.0 + power)


def smoothing_iteration(
    present_warmth,
    present_moisture,
    excess_warmth,
    pore_moisture,
    cement_maturity_degree,
    warmth_around,
    moisture_around,
):
    chemical_progress = cement_maturing_speed(
        present_warmth, present_moisture, cement_maturity_degree
    )
    emitted_warmth_total = (
        warmth_around[0]
        + warmth_around[1]
        + warmth_around[2]
        + warmth_around[3]
        + warmth_around[4]
        + warmth_around[5]
    )
    warmth_after = (
        excess_warmth + cement_warmth_output * chemical_progress + emitted_warmth_total
    ) / 7.0
    own_diff = diffusivity(present_moisture)
    conduct = jnp.zeros_like(present_moisture)
    inflow = jnp.zeros_like(present_moisture)
    for neighbour in moisture_around:
        face_diff = 0.5 * (own_diff + diffusivity(neighbour))
        conduct = conduct + face_diff
        inflow = inflow + face_diff * neighbour
    moisture_after = (pore_moisture - desiccation * chemical_progress + inflow) / (1.0 + conduct)
    return (warmth_after, moisture_after)


def viscous_strain_advance(
    loading_tension,
    field_temp,
    field_hum,
    parcel_maturity,
    poured_tally,
    series_prior,
    micro_tension_before,
):
    factor = jnp.exp(creep_activation * field_temp) * (0.1 + 0.9 * field_hum * field_hum)
    lifetimes = 0.1 * 3.0 ** jnp.arange(series_prior.shape[-2]).astype(jnp.float32)
    decays = jnp.exp(-factor[..., None, :] / lifetimes[:, None])
    chain_new = decays * series_prior + kelvin_amp * (1.0 - decays) * loading_tension[..., None, :]
    solidify = jnp.sqrt(age_scale / parcel_maturity) + 0.2
    kelvin_part = solidify * jnp.sum(chain_new - series_prior, axis=-2)
    prestress_next = micro_tension_before / (1.0 + micro_rate * factor * micro_tension_before)
    flow_part = flow_coef * factor * prestress_next * loading_tension
    position = jnp.arange(loading_tension.shape[-1]).astype(jnp.float32)
    placed = position < poured_tally
    series_result = jnp.where(placed[..., None, :], chain_new, series_prior)
    micro_tension_result = jnp.where(placed, prestress_next, micro_tension_before)
    small_change = jnp.where(placed, kelvin_part + flow_part, jnp.zeros_like(loading_tension))
    return (series_result, micro_tension_result, small_change)


def surrounding_entries(stacked, vertical_index):
    local_verticals = stacked.shape[2]
    z_padded = with_halo(stacked, (("gz", 1),), 1)
    y_padded = with_halo(stacked, (("gy", 2),), NX)
    upper_cell = z_padded[:, 2:, :]
    lower_cell = z_padded[:, :-2, :]
    north_cell = y_padded[:, :, 2 * NX : 2 * NX + local_verticals]
    south_cell = y_padded[:, :, 0:local_verticals]
    east_cell = jnp.where(
        vertical_index < NX - 1, jnp.pad(stacked[:, :, 1:], ((0, 0), (0, 0), (0, 1))), 0.0
    )
    west_cell = jnp.where(
        vertical_index > 0, jnp.pad(stacked[:, :, :-1], ((0, 0), (0, 0), (1, 0))), 0.0
    )
    return (upper_cell, lower_cell, north_cell, south_cell, east_cell, west_cell)


def body(
    excess_warmth,
    pore_moisture,
    cement_maturity_degree,
    parcel_filled_tally,
    parcel_keeper_position,
    layer_pouring_times,
    voigt_strains_stored,
    micro_tension,
):
    local_horizontals, local_verticals = excess_warmth.shape
    vertical_index = jnp.arange(local_verticals) % NX
    present_warmth = excess_warmth
    present_moisture = pore_moisture
    for sweep_index in range(SWEEPS):
        flanking_everything = surrounding_entries(
            jnp.stack((present_warmth, present_moisture)), vertical_index
        )
        warmth_around = [volume_site[0] for volume_site in flanking_everything]
        moisture_around = [volume_site[1] for volume_site in flanking_everything]
        present_warmth, present_moisture = smoothing_iteration(
            present_warmth,
            present_moisture,
            excess_warmth,
            pore_moisture,
            cement_maturity_degree,
            warmth_around,
            moisture_around,
        )
    cement_maturity_after = cement_maturity_degree + cement_maturing_speed(
        present_warmth, present_moisture, cement_maturity_degree
    )
    loading_tension = -cement_maturity_after * (
        expansion_factor * present_warmth + drying_contraction_factor * (1.0 - present_moisture)
    )
    parcels_per_line = local_verticals // PARCEL_SITES
    lifts_dev = local_horizontals // LIFT
    start_lift = lax.axis_index("gz") * lifts_dev
    local_times = lax.dynamic_slice_in_dim(layer_pouring_times, start_lift, lifts_dev)
    row_age = now_hours - jnp.repeat(local_times, LIFT).astype(jnp.float32)
    block_ages = jnp.repeat(row_age, parcels_per_line)
    total_slots = voigt_strains_stored.shape[0]
    flat_slot = parcel_keeper_position.reshape(-1)
    payload = jnp.stack(
        (
            loading_tension.reshape(local_horizontals, parcels_per_line, PARCEL_SITES),
            present_warmth.reshape(local_horizontals, parcels_per_line, PARCEL_SITES),
            present_moisture.reshape(local_horizontals, parcels_per_line, PARCEL_SITES),
        ),
        axis=2,
    ).reshape(-1, 3, PARCEL_SITES)
    send_fields = jnp.zeros((total_slots, 3, PARCEL_SITES), jnp.float32).at[flat_slot].set(payload)
    send_count = (
        jnp.zeros((total_slots,), jnp.float32)
        .at[flat_slot]
        .set(parcel_filled_tally.reshape(-1).astype(jnp.float32))
    )
    send_age = jnp.ones((total_slots,), jnp.float32).at[flat_slot].set(block_ages)
    got_fields, got_count, got_age = (
        lax.all_to_all(send_fields, ("gz", "gy"), split_axis=0, concat_axis=0, tiled=True),
        lax.all_to_all(send_count, ("gz", "gy"), split_axis=0, concat_axis=0, tiled=True),
        lax.all_to_all(send_age, ("gz", "gy"), split_axis=0, concat_axis=0, tiled=True),
    )
    series_result, micro_tension_result, small_change = viscous_strain_advance(
        got_fields[:, 0],
        got_fields[:, 1],
        got_fields[:, 2],
        got_age[:, None],
        got_count[:, None],
        voigt_strains_stored,
        micro_tension,
    )
    returned = lax.all_to_all(small_change, ("gz", "gy"), split_axis=0, concat_axis=0, tiled=True)
    creep_cells = returned[flat_slot].reshape(local_horizontals, local_verticals)
    return (
        present_warmth,
        present_moisture,
        cement_maturity_after,
        creep_cells,
        series_result,
        micro_tension_result,
    )


def solution(mesh):
    in_specs = (
        P("gz", "gy"),
        P("gz", "gy"),
        P("gz", "gy"),
        P("gz", "gy"),
        P("gz", "gy"),
        P(),
        P(("gz", "gy"), None, None),
        P(("gz", "gy"), None),
    )
    out_specs = (
        P("gz", "gy"),
        P("gz", "gy"),
        P("gz", "gy"),
        P("gz", "gy"),
        P(("gz", "gy"), None, None),
        P(("gz", "gy"), None),
    )
    return jax.shard_map(body, mesh=mesh, in_specs=in_specs, out_specs=out_specs, check_vma=False)
```

profile of v0, /device:TPU:0, one launch (start us, length us, event | category | flops | bytes accessed | tf_op | source)
XLA Modules:
  0.0 273.0 jit_solution(6023286300258593316)
XLA Ops:
  1.6 2.4 collective-permute-start.3
  6.2 4.2 %collective-permute-start.1 = (f32[2,1,1536]{2,1,0:T(1,128)S(1)}, f32[2,1,1536]{2,1,0:T(1,128)S(1)}, u32[]{:S(2)}, u32[]{:S(2)}) collective-permute-start(f32[2,1,1536]{2,1,0:T(1,128)S(1)} %get-tuple-element.30), channel_id=1, source_target_pairs={{0,4},{4,8},{8,12},{12,16},{16,20},{20,24},{24,28},{1,5},{5,9},{9,... | collective-permute-start | bytes 36872 | tf_op jit(solution)/shard_map/ppermute | solution.py:36
  13.5 4.1 %scatter_custom_fusion = f32[1728]{0:T(1024)S(1)} fusion(s32[576]{0:T(1024)S(1)} %fusion.37, f32[576]{0:T(1024)S(1)} %reshape.154, f32[]{:T(128)} %constant.34.clone.1), kind=kCustom, calls=%fused_computation.135 | custom fusion | bytes 6916 | tf_op jit(solution)/shard_map/scatter | solution.py:196
  18.3 9.5 %all-to-all-start = ((f32[32,54,1]{1,2,0:T(1,128)}), f32[32,54,1]{1,2,0:T(1,128)S(1)}, u32[]{:S(2)}, u32[]{:S(2)}) async-start(f32[32,54,1]{1,2,0:T(1,128)} %bitcast.27), calls=%async_computation | async-start | bytes 32768 | tf_op jit(solution)/shard_map/all_to_all | solution.py:201
  30.9 4.1 %scatter_custom_fusion.1 = f32[1728]{0:T(1024)S(1)} fusion(s32[576]{0:T(1024)S(1)} %fusion.37, f32[576]{0:T(1024)S(1)} %reshape.162, f32[]{:T(128)} %constant.26.clone.1), kind=kCustom, calls=%fused_computation.133 | custom fusion | bytes 6916 | tf_op jit(solution)/shard_map/scatter | solution.py:198
  37.9 2.2 collective-permute-start.7
  41.3 3.6 %collective-permute-start.5 = (f32[2,1,1536]{2,1,0:T(1,128)S(1)}, f32[2,1,1536]{2,1,0:T(1,128)S(1)}, u32[]{:S(2)}, u32[]{:S(2)}) collective-permute-start(f32[2,1,1536]{2,1,0:T(1,128)S(1)} %get-tuple-element.26), channel_id=1, source_target_pairs={{0,4},{4,8},{8,12},{12,16},{16,20},{20,24},{24,28},{1,5},{5,9},{9,... | collective-permute-start | bytes 36872 | tf_op jit(solution)/shard_map/ppermute | solution.py:36
  46.3 4.2 %collective-permute-done.4 = f32[2,1,1536]{2,1,0:T(1,128)S(1)} collective-permute-done((f32[2,1,1536]{2,1,0:T(1,128)S(1)}, f32[2,1,1536]{2,1,0:T(1,128)S(1)}, u32[]{:S(2)}, u32[]{:S(2)}) %collective-permute-start.4) | collective-permute-done | bytes 12320 | tf_op jit(solution)/shard_map/ppermute | solution.py:38
  52.6 2.5 collective-permute-start.11
  56.4 4.3 %collective-permute-start.9 = (f32[2,1,1536]{2,1,0:T(1,128)S(1)}, f32[2,1,1536]{2,1,0:T(1,128)S(1)}, u32[]{:S(2)}, u32[]{:S(2)}) collective-permute-start(f32[2,1,1536]{2,1,0:T(1,128)S(1)} %get-tuple-element.22), channel_id=1, source_target_pairs={{0,4},{4,8},{8,12},{12,16},{16,20},{20,24},{24,28},{1,5},{5,9},{9,... | collective-permute-start | bytes 36872 | tf_op jit(solution)/shard_map/ppermute | solution.py:36
  62.1 4.2 %collective-permute-done.8 = f32[2,1,1536]{2,1,0:T(1,128)S(1)} collective-permute-done((f32[2,1,1536]{2,1,0:T(1,128)S(1)}, f32[2,1,1536]{2,1,0:T(1,128)S(1)}, u32[]{:S(2)}, u32[]{:S(2)}) %collective-permute-start.8) | collective-permute-done | bytes 12320 | tf_op jit(solution)/shard_map/ppermute | solution.py:38
  66.3 2.2 add_multiply_fusion
  68.7 8.9 %all-to-all-start.1 = ((f32[32,54,1]{1,2,0:T(1,128)}), f32[32,54,1]{1,2,0:T(1,128)}, u32[]{:S(2)}, u32[]{:S(2)}) async-start(f32[32,54,1]{1,2,0:T(1,128)} %bitcast.28), calls=%async_computation.1 | async-start | bytes 32768 | tf_op jit(solution)/shard_map/all_to_all | solution.py:202
  78.4 2.0 broadcast_in_dim.70
  80.4 58.0 %scatter_fusion = f32[1728,3,128]{2,1,0:T(4,128)} fusion(f32[1728,3,128]{2,1,0:T(4,128)} %broadcast_in_dim.70, s32[576]{0:T(1024)S(1)} %fusion.37, f32[576,3,128]{2,1,0:T(4,128)S(1)} %pad_maximum_fusion), kind=kCustom, calls=%fused_computation.3 | custom fusion | bytes 2656512 | tf_op jit(solution)/shard_map/scatter | solution.py:192
  138.4 5.6 %all-to-all-start.2 = ((f32[1728,3,128]{2,1,0:T(4,128)}), f32[1728,3,128]{2,1,0:T(4,128)S(1)}, u32[]{:S(2)}, u32[]{:S(2)}) async-start(f32[1728,3,128]{2,1,0:T(4,128)} %scatter_fusion), calls=%async_computation.2 | async-start | bytes 7077888 | tf_op jit(solution)/shard_map/all_to_all | solution.py:200
  150.0 1.6 broadcast_compare_fusion
  151.6 72.6 %all-to-all-done.2 = f32[1728,3,128]{2,1,0:T(4,128)S(1)} async-done(((f32[1728,3,128]{2,1,0:T(4,128)}), f32[1728,3,128]{2,1,0:T(4,128)S(1)}, u32[]{:S(2)}, u32[]{:S(2)}) %all-to-all-start.2) | async-done | bytes 2654240 | tf_op jit(solution)/shard_map/all_to_all | solution.py:200
  224.2 1.8 fusion.41
  227.0 12.5 %fusion = (f32[1728,8,128]{2,1,0:T(8,128)}, f32[1728,128]{1,0:T(8,128)S(1)}) fusion(f32[1728,8,128]{2,1,0:T(8,128)} %param.14, f32[1728,128]{1,0:T(8,128)S(1)} %broadcast_multiply_fusion, f32[8]{0:T(128)S(1)} %copy-done.10, f32[1728,128]{1,0:T(8,128)S(1)} %fusion.4, pred[1728,128]{1,0:T(8,128)(4,1)S(1)} %copy-done.6), kind=kLoop, calls=%fused_computation.7 | loop fusion | flops 13934592 | bytes 17031200 | tf_op jit(solution)/shard_map/jit(_where)/select_n | solution.py:118
  239.6 1.9 compare_select_fusion
  242.5 4.7 %all-to-all-start.3 = ((f32[32,54,128]{2,1,0:T(8,128)}), f32[32,54,128]{2,1,0:T(8,128)S(1)}, u32[]{:S(2)}, u32[]{:S(2)}) async-start(f32[32,54,128]{2,1,0:T(8,128)} %all_to_all.28), calls=%async_computation.3 | async-start | bytes 1835008 | tf_op jit(solution)/shard_map/all_to_all | solution.py:213
  247.2 23.4 %all-to-all-done.3 = f32[32,54,128]{2,1,0:T(8,128)S(1)} async-done(((f32[32,54,128]{2,1,0:T(8,128)}), f32[32,54,128]{2,1,0:T(8,128)S(1)}, u32[]{:S(2)}, u32[]{:S(2)}) %all-to-all-start.3) | async-done | bytes 884768 | tf_op jit(solution)/shard_map/all_to_all | solution.py:213
  270.7 1.6 gather_fusion
  (93 shorter events, 29.7 us)
Async XLA Ops:
  0.6 35.1 %copy-start.1 = (f32[48,1536]{1,0:T(8,128)S(1)}, f32[48,1536]{1,0:T(8,128)}, u32[]{:S(2)}) copy-start(f32[48,1536]{1,0:T(8,128)} %param.9) | copy-start | bytes 884740
  0.6 35.1 %copy-start = (f32[48,1536]{1,0:T(8,128)S(1)}, f32[48,1536]{1,0:T(8,128)}, u32[]{:S(2)}) copy-start(f32[48,1536]{1,0:T(8,128)} %param.8) | copy-start | bytes 884740
  0.7 29.8 %copy-start.11 = (s32[48]{0:T(128)S(1)}, s32[48]{0:T(128)}, u32[]{:S(2)}) copy-start(s32[48]{0:T(128)} %param.13) | copy-start | bytes 580
  0.7 35.1 %copy-start.2 = (f32[48,1536]{1,0:T(8,128)S(1)}, f32[48,1536]{1,0:T(8,128)}, u32[]{:S(2)}) copy-start(f32[48,1536]{1,0:T(8,128)} %param.10) | copy-start | bytes 884740
  1.6 34.1 %collective-permute-start.3 = (f32[2,48,48]{2,1,0:T(8,128)S(1)}, f32[2,48,48]{2,1,0:T(8,128)S(1)}, u32[]{:S(2)}, u32[]{:S(2)}) collective-permute-start(f32[2,48,48]{2,1,0:T(8,128)S(1)} %get-tuple-element.32), channel_id=1, source_target_pairs={{0,1},{1,2},{2,3},{4,5},{5,6},{6,7},{8,9},{9,10},{10,11},{12,13},{... | collective-permute-start | bytes 55304 | tf_op jit(solution)/shard_map/ppermute | solution.py:36
  4.0 31.8 %collective-permute-start.2 = (f32[2,48,48]{2,1,0:T(8,128)S(1)}, f32[2,48,48]{2,1,0:T(8,128)S(1)}, u32[]{:S(2)}, u32[]{:S(2)}) collective-permute-start(f32[2,48,48]{2,1,0:T(8,128)S(1)} %get-tuple-element.31), channel_id=1, source_target_pairs={{1,0},{2,1},{3,2},{5,4},{6,5},{7,6},{9,8},{10,9},{11,10},{13,12},{... | collective-permute-start | bytes 55304 | tf_op jit(solution)/shard_map/ppermute | solution.py:38
  6.2 29.6 %collective-permute-start.1 = (f32[2,1,1536]{2,1,0:T(1,128)S(1)}, f32[2,1,1536]{2,1,0:T(1,128)S(1)}, u32[]{:S(2)}, u32[]{:S(2)}) collective-permute-start(f32[2,1,1536]{2,1,0:T(1,128)S(1)} %get-tuple-element.30), channel_id=1, source_target_pairs={{0,4},{4,8},{8,12},{12,16},{16,20},{20,24},{24,28},{1,5},{5,9},{9,... | collective-permute-start | bytes 36872 | tf_op jit(solution)/shard_map/ppermute | solution.py:36
  10.4 25.3 %collective-permute-start = (f32[2,1,1536]{2,1,0:T(1,128)S(1)}, f32[2,1,1536]{2,1,0:T(1,128)S(1)}, u32[]{:S(2)}, u32[]{:S(2)}) collective-permute-start(f32[2,1,1536]{2,1,0:T(1,128)S(1)} %get-tuple-element.29), channel_id=1, source_target_pairs={{4,0},{8,4},{12,8},{16,12},{20,16},{24,20},{28,24},{5,1},{9,5},{13... | collective-permute-start | bytes 36872 | tf_op jit(solution)/shard_map/ppermute | solution.py:38
  12.6 67.8 %copy-start.7 = (s32[576]{0:T(1024)}, s32[576]{0:T(1024)S(1)}, u32[]{:S(2)}) copy-start(s32[576]{0:T(1024)S(1)} %fusion.37) | copy-start | bytes 6916
  18.3 50.3 %all-to-all-start = ((f32[32,54,1]{1,2,0:T(1,128)}), f32[32,54,1]{1,2,0:T(1,128)S(1)}, u32[]{:S(2)}, u32[]{:S(2)}) async-start(f32[32,54,1]{1,2,0:T(1,128)} %bitcast.27), calls=%async_computation | async-start | bytes 32768 | tf_op jit(solution)/shard_map/all_to_all | solution.py:201
  37.9 12.6 %collective-permute-start.7 = (f32[2,48,48]{2,1,0:T(8,128)S(1)}, f32[2,48,48]{2,1,0:T(8,128)S(1)}, u32[]{:S(2)}, u32[]{:S(2)}) collective-permute-start(f32[2,48,48]{2,1,0:T(8,128)S(1)} %get-tuple-element.28), channel_id=1, source_target_pairs={{0,1},{1,2},{2,3},{4,5},{5,6},{6,7},{8,9},{9,10},{10,11},{12,13},{... | collective-permute-start | bytes 55304 | tf_op jit(solution)/shard_map/ppermute | solution.py:36
  40.0 10.5 %collective-permute-start.6 = (f32[2,48,48]{2,1,0:T(8,128)S(1)}, f32[2,48,48]{2,1,0:T(8,128)S(1)}, u32[]{:S(2)}, u32[]{:S(2)}) collective-permute-start(f32[2,48,48]{2,1,0:T(8,128)S(1)} %get-tuple-element.27), channel_id=1, source_target_pairs={{1,0},{2,1},{3,2},{5,4},{6,5},{7,6},{9,8},{10,9},{11,10},{13,12},{... | collective-permute-start | bytes 55304 | tf_op jit(solution)/shard_map/ppermute | solution.py:38
  41.3 5.0 %collective-permute-start.5 = (f32[2,1,1536]{2,1,0:T(1,128)S(1)}, f32[2,1,1536]{2,1,0:T(1,128)S(1)}, u32[]{:S(2)}, u32[]{:S(2)}) collective-permute-start(f32[2,1,1536]{2,1,0:T(1,128)S(1)} %get-tuple-element.26), channel_id=1, source_target_pairs={{0,4},{4,8},{8,12},{12,16},{16,20},{20,24},{24,28},{1,5},{5,9},{9,... | collective-permute-start | bytes 36872 | tf_op jit(solution)/shard_map/ppermute | solution.py:36
  44.9 5.6 %collective-permute-start.4 = (f32[2,1,1536]{2,1,0:T(1,128)S(1)}, f32[2,1,1536]{2,1,0:T(1,128)S(1)}, u32[]{:S(2)}, u32[]{:S(2)}) collective-permute-start(f32[2,1,1536]{2,1,0:T(1,128)S(1)} %get-tuple-element.25), channel_id=1, source_target_pairs={{4,0},{8,4},{12,8},{16,12},{20,16},{24,20},{28,24},{5,1},{9,5},{13... | collective-permute-start | bytes 36872 | tf_op jit(solution)/shard_map/ppermute | solution.py:38
  52.6 13.7 %collective-permute-start.11 = (f32[2,48,48]{2,1,0:T(8,128)S(1)}, f32[2,48,48]{2,1,0:T(8,128)S(1)}, u32[]{:S(2)}, u32[]{:S(2)}) collective-permute-start(f32[2,48,48]{2,1,0:T(8,128)S(1)} %get-tuple-element.24), channel_id=1, source_target_pairs={{0,1},{1,2},{2,3},{4,5},{5,6},{6,7},{8,9},{9,10},{10,11},{12,13},{... | collective-permute-start | bytes 55304 | tf_op jit(solution)/shard_map/ppermute | solution.py:36
  55.1 11.2 %collective-permute-start.10 = (f32[2,48,48]{2,1,0:T(8,128)S(1)}, f32[2,48,48]{2,1,0:T(8,128)S(1)}, u32[]{:S(2)}, u32[]{:S(2)}) collective-permute-start(f32[2,48,48]{2,1,0:T(8,128)S(1)} %get-tuple-element.23), channel_id=1, source_target_pairs={{1,0},{2,1},{3,2},{5,4},{6,5},{7,6},{9,8},{10,9},{11,10},{13,12},{... | collective-permute-start | bytes 55304 | tf_op jit(solution)/shard_map/ppermute | solution.py:38
  56.4 5.7 %collective-permute-start.9 = (f32[2,1,1536]{2,1,0:T(1,128)S(1)}, f32[2,1,1536]{2,1,0:T(1,128)S(1)}, u32[]{:S(2)}, u32[]{:S(2)}) collective-permute-start(f32[2,1,1536]{2,1,0:T(1,128)S(1)} %get-tuple-element.22), channel_id=1, source_target_pairs={{0,4},{4,8},{8,12},{12,16},{16,20},{20,24},{24,28},{1,5},{5,9},{9,... | collective-permute-start | bytes 36872 | tf_op jit(solution)/shard_map/ppermute | solution.py:36
  60.7 5.6 %collective-permute-start.8 = (f32[2,1,1536]{2,1,0:T(1,128)S(1)}, f32[2,1,1536]{2,1,0:T(1,128)S(1)}, u32[]{:S(2)}, u32[]{:S(2)}) collective-permute-start(f32[2,1,1536]{2,1,0:T(1,128)S(1)} %get-tuple-element.21), channel_id=1, source_target_pairs={{4,0},{8,4},{12,8},{16,12},{20,16},{24,20},{28,24},{5,1},{9,5},{13... | collective-permute-start | bytes 36872 | tf_op jit(solution)/shard_map/ppermute | solution.py:38
  68.6 9.0 %copy-start.3 = (f32[48,1536]{1,0:T(8,128)}, f32[48,1536]{1,0:T(8,128)S(1)}, u32[]{:S(2)}) copy-start(f32[48,1536]{1,0:T(8,128)S(1)} %get-tuple-element.8) | copy-start | bytes 884740
  68.7 69.7 %all-to-all-start.1 = ((f32[32,54,1]{1,2,0:T(1,128)}), f32[32,54,1]{1,2,0:T(1,128)}, u32[]{:S(2)}, u32[]{:S(2)}) async-start(f32[32,54,1]{1,2,0:T(1,128)} %bitcast.28), calls=%async_computation.1 | async-start | bytes 32768 | tf_op jit(solution)/shard_map/all_to_all | solution.py:202
  138.4 85.8 %all-to-all-start.2 = ((f32[1728,3,128]{2,1,0:T(4,128)}), f32[1728,3,128]{2,1,0:T(4,128)S(1)}, u32[]{:S(2)}, u32[]{:S(2)}) async-start(f32[1728,3,128]{2,1,0:T(4,128)} %scatter_fusion), calls=%async_computation.2 | async-start | bytes 7077888 | tf_op jit(solution)/shard_map/all_to_all | solution.py:200
  227.0 12.5 %copy-start.5 = (f32[1728,128]{1,0:T(8,128)S(1)}, f32[1728,128]{1,0:T(8,128)}, u32[]{:S(2)}) copy-start(f32[1728,128]{1,0:T(8,128)} %param.15) | copy-start | bytes 2654212
  227.0 12.5 %copy-start.9 = (f32[128]{0:T(128)S(1)}, f32[128]{0:T(128)}, u32[]{:S(2)}) copy-start(f32[128]{0:T(128)} %iota_convert_fusion) | copy-start | bytes 1540
  242.5 28.1 %all-to-all-start.3 = ((f32[32,54,128]{2,1,0:T(8,128)}), f32[32,54,128]{2,1,0:T(8,128)S(1)}, u32[]{:S(2)}, u32[]{:S(2)}) async-start(f32[32,54,128]{2,1,0:T(8,128)} %all_to_all.28), calls=%async_computation.3 | async-start | bytes 1835008 | tf_op jit(solution)/shard_map/all_to_all | solution.py:213
  (4 other events, 18.5 us)
where the time goes:
time: 275 us; the launch traced here: 273 us
  waiting for transfers between devices  104 us (38%)
  local copies, waits for them, and re-layouts  79.2 us (29%)
  starting transfers between devices  55.6 us (20%)
  other arithmetic  32.7 us (12%)
    all_to_all x1, waiting for transfers between devices, body(): lax.all_to_all(send_fields, ('gz', 'gy'), split_axis=0, concat_axis=0, ti...  72.6 us
    scatter x1, local copies, waits for them, and re-layouts, body(): jnp.zeros((total_slots, 3, PARCEL_SITES), jnp.float32).at[flat_slot]  58 us
    all_to_all x1, waiting for transfers between devices, body(): lax.all_to_all(small_change, ('gz', 'gy'), split_axis=0, concat_axis=0, t...  23.4 us
    ppermute x6, starting transfers between devices, with_halo(): lax.ppermute(tail, axis, [(i, (i + 1) % count) for i in range(ends)])  19.1 us
    select_n x1, other arithmetic, viscous_strain_advance(): series_result = jnp.where(placed[..., None, :], chain_new, series_prior)  12.5 us
    all_to_all x1, starting transfers between devices, body(): lax.all_to_all(send_count, ('gz', 'gy'), split_axis=0, concat_axis=0, til...  9.53 us
    all_to_all x1, starting transfers between devices, body(): lax.all_to_all(send_age, ('gz', 'gy'), split_axis=0, concat_axis=0, tiled...  8.89 us
    ppermute x6, waiting for transfers between devices, with_halo(): lax.ppermute(head, axis, [((i + 1) % count, i) for i in range(ends)])  8.41 us
  transfers between devices with their start and end apart: 16, of which 4 were waited for; matrix products, arithmetic and copies ran while one was open for 33% of the time, Pallas kernels for 0%

commit v1 on v0

v1 whole, which is shorter than its diff:
```python
import functools

import jax
import jax.numpy as jnp
from jax import lax
from jax.experimental import pallas as pl
from jax.experimental.pallas import tpu as pltpu
from jax.sharding import PartitionSpec as P

NX = 48
SITES = 128
KU = 8
SWEEPS = 3
LIFT = 8
PAD = 128
TOP = 8
GROUP = 4
DRY = 0.05 + 0.95 / (1.0 + 5.0**16)
MESH = pl.DeviceIdType.MESH


def rate(temp, hum, degree):
    term = 7.5 - 7.5 * hum
    term = term * term
    return 0.05 * (1.0 - degree) * jnp.exp(0.5 * temp) / (1.0 + term * term)


def diffusivity(hum):
    ratio = 5.0 * (1.0 - hum)
    power = ratio * ratio
    power = power * power
    power = power * power
    power = power * power
    return 0.05 + 0.95 / (1.0 + power)


def padded_rows(count):
    return -(-count // 8) * 8


def greet_all(n, n_gy, me):
    barrier = pltpu.get_barrier_semaphore()

    def greet(j, carry):
        other = lax.rem(me + 1 + j, n)
        pl.semaphore_signal(
            barrier, inc=1, device_id=(other // n_gy, lax.rem(other, n_gy)), device_id_type=MESH
        )
        return carry

    lax.fori_loop(0, n - 1, greet, 0)
    pl.semaphore_wait(barrier, n - 1)


def partner(i, n, me):
    return lax.rem(me + 1 + lax.rem(i + n // 2 - 1, n - 1), n)


def sweep_and_send(
    n_gz, n_gy, cap,
    warmth, moisture, degree, tally, index, solid,
    temp_out, hum_out, degree_out, got,
    ext, diff, z_send, z_recv, blocks, send, z_sems, y_sems, out_sems, in_sems, own_sem,
):
    n = n_gz * n_gy
    rows, cols = warmth.shape
    wide = cols + 2 * PAD
    per_row = cols // SITES
    cp = padded_rows(cap + 1)
    gz = lax.axis_index("gz")
    gy = lax.axis_index("gy")
    me = gz * n_gy + gy
    greet_all(n, n_gy, me)

    x = lax.rem(lax.broadcasted_iota(jnp.int32, (8, cols), 1), NX)
    has_west = x > 0
    has_east = x < NX - 1
    inner = slice(PAD, PAD + cols)
    body_rows = slice(TOP, TOP + rows)

    ext[0, 0, body_rows, inner] = warmth[...]
    ext[0, 1, body_rows, inner] = moisture[...]

    for s in range(SWEEPS):
        for f in range(2):
            z_send[s, 0, f : f + 1] = ext[s, f, TOP : TOP + 1, inner]
            z_send[s, 1, f : f + 1] = ext[s, f, TOP + rows - 1 : TOP + rows, inner]

        def z_copy(side, s=s):
            to = gz - 1 + 2 * side
            return pltpu.make_async_remote_copy(
                src_ref=z_send.at[s, side],
                dst_ref=z_recv.at[s, 1 - side],
                send_sem=z_sems.at[s, 0, side],
                recv_sem=z_sems.at[s, 1, 1 - side],
                device_id=(to, gy),
                device_id_type=MESH,
            )

        def y_copy(side, s=s):
            to = gy - 1 + 2 * side
            a = PAD if side == 0 else cols
            b = PAD + cols if side == 0 else 0
            return pltpu.make_async_remote_copy(
                src_ref=ext.at[s, :, body_rows, pl.ds(a, PAD)],
                dst_ref=ext.at[s, :, body_rows, pl.ds(b, PAD)],
                send_sem=y_sems.at[s, 0, side],
                recv_sem=y_sems.at[s, 1, 1 - side],
                device_id=(gz, to),
                device_id_type=MESH,
            )

        there = (gz > 0, gz < n_gz - 1)
        beside = (gy > 0, gy < n_gy - 1)
        for side in range(2):
            pl.when(beside[side])(lambda side=side: y_copy(side).start())
            pl.when(there[side])(lambda side=side: z_copy(side).start())

        for side in range(2):

            @pl.when(jnp.logical_not(there[side]))
            def _(side=side, s=s):
                z_recv[s, side] = jnp.zeros((2, cols), jnp.float32)

            @pl.when(jnp.logical_not(beside[side]))
            def _(side=side, s=s):
                b = 0 if side == 0 else PAD + cols
                ext[s, :, body_rows, pl.ds(b, PAD)] = jnp.zeros((2, rows, PAD), jnp.float32)

        for side in range(2):
            pl.when(there[side])(lambda side=side: z_copy(1 - side).wait_recv())
            pl.when(beside[side])(lambda side=side: y_copy(1 - side).wait_recv())

        for f in range(2):
            ext[s, f, TOP - 1 : TOP, inner] = z_recv[s, 0, f : f + 1]
            ext[s, f, TOP + rows : TOP + rows + 1, inner] = z_recv[s, 1, f : f + 1]
        diff[TOP - 1 : TOP, inner] = diffusivity(z_recv[s, 0, 1:2])
        diff[TOP + rows : TOP + rows + 1, inner] = diffusivity(z_recv[s, 1, 1:2])
        for r in range(0, rows, 8):
            here = slice(TOP + r, TOP + r + 8)
            diff[here, :] = diffusivity(ext[s, 1, here, :])

        for r in range(0, rows, 8):
            here = slice(TOP + r, TOP + r + 8)
            up = slice(TOP + r + 1, TOP + r + 9)
            down = slice(TOP + r - 1, TOP + r + 7)
            own = slice(r, r + 8)
            temp = ext[s, 0, here, :]
            hum = ext[s, 1, here, :]
            cond = diff[here, :]

            def aside(v, shift):
                return pltpu.roll(v, shift % wide, 1)[:, inner]

            total = (
                ext[s, 0, up, inner] + ext[s, 0, down, inner] + aside(temp, -NX) + aside(temp, NX)
            )
            total = total + jnp.where(has_east, aside(temp, -1), 0.0)
            total = total + jnp.where(has_west, aside(temp, 1), 0.0)
            t0 = temp[:, inner]
            h0 = hum[:, inner]
            d0 = cond[:, inner]
            progress = rate(t0, h0, degree[own, :])
            near = [
                (ext[s, 1, up, inner], diff[up, inner]),
                (ext[s, 1, down, inner], diff[down, inner]),
                (aside(hum, -NX), aside(cond, -NX)),
                (aside(hum, NX), aside(cond, NX)),
                (
                    jnp.where(has_east, aside(hum, -1), 0.0),
                    jnp.where(has_east, aside(cond, -1), DRY),
                ),
                (
                    jnp.where(has_west, aside(hum, 1), 0.0),
                    jnp.where(has_west, aside(cond, 1), DRY),
                ),
            ]
            conduct = None
            inflow = None
            for g, dg in near:
                c = 0.5 * (d0 + dg)
                conduct = c if conduct is None else conduct + c
                inflow = c * g if inflow is None else inflow + c * g
            t1 = (warmth[own, :] + 4.0 * progress + total) / 7.0
            h1 = (moisture[own, :] - 0.5 * progress + inflow) / (1.0 + conduct)
            if s < SWEEPS - 1:
                ext[s + 1, 0, here, inner] = t1
                ext[s + 1, 1, here, inner] = h1
            else:
                temp_out[own, :] = t1
                hum_out[own, :] = h1
                a1 = degree[own, :] + rate(t1, h1, degree[own, :])
                degree_out[own, :] = a1
                stress = -a1 * (0.5 * t1 + 2.0 * (1.0 - h1))
                phi = jnp.exp(0.3 * t1) * (0.1 + 0.9 * h1 * h1)
                lane = lax.broadcasted_iota(jnp.int32, (8, SITES), 1)
                for j in range(per_row):
                    cut = slice(j * SITES, (j + 1) * SITES)
                    at = slice(j * rows + r, j * rows + r + 8)
                    placed = lane < tally[own, j : j + 1]
                    blocks[0, at, :] = jnp.where(placed, phi[:, cut], 0.0)
                    blocks[1, at, :] = jnp.where(placed, stress[:, cut], 0.0)

    nb = rows * per_row
    blocks[0, nb : nb + 8, :] = jnp.zeros((8, SITES), jnp.float32)
    blocks[1, nb : nb + 8, :] = jnp.zeros((8, SITES), jnp.float32)

    def copy_to(i, o):
        return pltpu.make_async_remote_copy(
            src_ref=send.at[o],
            dst_ref=got.at[me],
            send_sem=out_sems.at[o],
            recv_sem=in_sems.at[me],
            device_id=(o // n_gy, lax.rem(o, n_gy)),
            device_id_type=MESH,
        )

    def fill(o):
        for l in range(cap):
            k = index[o * cap + l]
            send[o, l : l + 1, :] = blocks[0, pl.ds(k, 1), :]
            send[o, cp + l : cp + l + 1, :] = blocks[1, pl.ds(k, 1), :]
        send[o, cap : cap + 1, :] = solid[pl.ds(o, 1), :]

    def push(i, carry):
        o = partner(i, n, me)
        fill(o)
        copy_to(i, o).start()
        return carry

    lax.fori_loop(0, n - 1, push, 0)
    fill(me)
    own_copy = pltpu.make_async_copy(send.at[me], got.at[me], own_sem)
    own_copy.start()

    for s in range(SWEEPS):
        for side in range(2):
            a = PAD if side == 0 else cols
            pl.when((gz > 0, gz < n_gz - 1)[side])(
                lambda s=s, side=side: pltpu.make_async_remote_copy(
                    src_ref=z_send.at[s, side],
                    dst_ref=z_recv.at[s, 1 - side],
                    send_sem=z_sems.at[s, 0, side],
                    recv_sem=z_sems.at[s, 1, 1 - side],
                    device_id=(gz - 1 + 2 * side, gy),
                    device_id_type=MESH,
                ).wait_send()
            )
            pl.when((gy > 0, gy < n_gy - 1)[side])(
                lambda s=s, side=side, a=a: pltpu.make_async_remote_copy(
                    src_ref=ext.at[s, :, body_rows, pl.ds(a, PAD)],
                    dst_ref=ext.at[s, :, body_rows, pl.ds(a, PAD)],
                    send_sem=y_sems.at[s, 0, side],
                    recv_sem=y_sems.at[s, 1, 1 - side],
                    device_id=(gz, gy - 1 + 2 * side),
                    device_id_type=MESH,
                ).wait_send()
            )

    own_copy.wait()

    def finish(i, carry):
        o = partner(i, n, me)
        pltpu.make_async_remote_copy(
            src_ref=send.at[o],
            dst_ref=got.at[o],
            send_sem=out_sems.at[o],
            recv_sem=in_sems.at[o],
            device_id=(o // n_gy, lax.rem(o, n_gy)),
            device_id_type=MESH,
        ).wait()
        return carry

    lax.fori_loop(0, n - 1, finish, 0)


def creep(cap, got, chain, micro, chain_out, micro_out, change):
    cp = padded_rows(cap + 1)
    unit = lax.broadcasted_iota(jnp.int32, (KU, SITES), 0)
    speed = jnp.full((KU, SITES), -10.0, jnp.float32)
    for m in range(1, KU):
        speed = jnp.where(unit == m, -10.0 / 3.0**m, speed)
    sub = lax.broadcasted_iota(jnp.int32, (cap, SITES), 0)
    lane = lax.broadcasted_iota(jnp.int32, (cap, SITES), 1)
    for q in range(GROUP):
        base = q * cap
        phi = got[q, 0:cap, :]
        stress = got[q, cp : cp + cap, :]
        row = got[q, cap : cap + 1, :]
        solid = jnp.sum(jnp.where(sub == lane, row, 0.0), axis=1, keepdims=True)
        s0 = micro[base : base + cap, :]
        s1 = s0 / (1.0 + 0.2 * phi * s0)
        micro_out[base : base + cap, :] = s1
        flow = 0.1 * phi * s1 * stress
        for l0 in range(0, cap, 8):
            l1 = min(l0 + 8, cap)
            old = chain[base + l0 : base + l1]
            decay = jnp.exp(phi[l0:l1][:, None, :] * speed[None])
            new = decay * old + 0.15 * (1.0 - decay) * stress[l0:l1][:, None, :]
            chain_out[base + l0 : base + l1] = new
            kelvin = jnp.sum(new - old, axis=1)
            change[q, l0:l1, :] = solid[l0:l1] * kelvin + flow[l0:l1]
        change[q, cap:cp, :] = jnp.zeros((cp - cap, SITES), jnp.float32)


def send_back(n_gz, n_gy, change, where, out, back, out_sems, in_sems):
    n = n_gz * n_gy
    rows, cols = out.shape
    cp = change.shape[1]
    me = lax.axis_index("gz") * n_gy + lax.axis_index("gy")
    greet_all(n, n_gy, me)

    def push(i, carry):
        o = partner(i, n, me)
        pltpu.make_async_remote_copy(
            src_ref=change.at[o],
            dst_ref=back.at[pl.ds(pl.multiple_of(me * cp, 8), cp)],
            send_sem=out_sems.at[o],
            recv_sem=in_sems.at[me],
            device_id=(o // n_gy, lax.rem(o, n_gy)),
            device_id_type=MESH,
        ).start()
        return carry

    lax.fori_loop(0, n - 1, push, 0)
    back[pl.ds(pl.multiple_of(me * cp, 8), cp), :] = change[me]

    def finish(i, carry):
        o = partner(i, n, me)
        pltpu.make_async_remote_copy(
            src_ref=change.at[o],
            dst_ref=back.at[pl.ds(pl.multiple_of(o * cp, 8), cp)],
            send_sem=out_sems.at[o],
            recv_sem=in_sems.at[o],
            device_id=(o // n_gy, lax.rem(o, n_gy)),
            device_id_type=MESH,
        ).wait()
        return carry

    lax.fori_loop(0, n - 1, finish, 0)
    per_row = cols // SITES

    def place(g, carry):
        r = pl.multiple_of(g * 8, 8)
        for j in range(per_row):
            lines = [back[pl.ds(where[(r + k) * per_row + j], 1), :] for k in range(8)]
            out[pl.ds(r, 8), j * SITES : (j + 1) * SITES] = jnp.concatenate(lines, axis=0)
        return carry

    lax.fori_loop(0, rows // 8, place, 0)


def body(n_gz, n_gy, warmth, moisture, degree, tally, keeper, pouring, chain, micro):
    n = n_gz * n_gy
    rows, cols = warmth.shape
    per_row = cols // SITES
    slots = chain.shape[0]
    cap = slots // n
    cp = padded_rows(cap + 1)
    nb = rows * per_row
    lifts = rows // LIFT
    vm = pl.BlockSpec(memory_space=pltpu.VMEM)
    sm = pl.BlockSpec(memory_space=pltpu.SMEM)
    hbm = pl.BlockSpec(memory_space=pl.ANY)
    f32 = jnp.float32

    local_times = lax.dynamic_slice_in_dim(pouring, lax.axis_index("gz") * lifts, lifts)
    age = 2400.0 - jnp.repeat(local_times, LIFT).astype(f32)
    solid = jnp.sqrt(600.0 / age) + 0.2
    flat = keeper.reshape(-1)
    hit = flat[None, :] == jnp.arange(slots, dtype=jnp.int32)[:, None]
    block = jnp.arange(nb, dtype=jnp.int32)
    held = (block % per_row) * rows + block // per_row
    index = nb + jnp.sum(jnp.where(hit, held[None, :] - nb, 0), axis=1)
    solid_slot = jnp.sum(jnp.where(hit, jnp.repeat(solid, per_row)[None, :], 0.0), axis=1)
    solid_rows = jnp.pad(solid_slot.reshape(n, cap), ((0, 0), (0, SITES - cap)))
    where = (flat // cap) * cp + flat % cap

    field = jax.ShapeDtypeStruct((rows, cols), f32)
    temp, hum, degree_after, got = pl.pallas_call(
        functools.partial(sweep_and_send, n_gz, n_gy, cap),
        out_shape=(field, field, field, jax.ShapeDtypeStruct((n, 2 * cp, SITES), f32)),
        in_specs=[vm, vm, vm, vm, sm, vm],
        out_specs=(vm, vm, vm, hbm),
        scratch_shapes=[
            pltpu.VMEM((SWEEPS, 2, rows + 2 * TOP, cols + 2 * PAD), f32),
            pltpu.VMEM((rows + 2 * TOP, cols + 2 * PAD), f32),
            pltpu.VMEM((SWEEPS, 2, 2, cols), f32),
            pltpu.VMEM((SWEEPS, 2, 2, cols), f32),
            pltpu.VMEM((2, nb + 8, SITES), f32),
            pltpu.VMEM((n, 2 * cp, SITES), f32),
            pltpu.SemaphoreType.DMA((SWEEPS, 2, 2)),
            pltpu.SemaphoreType.DMA((SWEEPS, 2, 2)),
            pltpu.SemaphoreType.DMA((n,)),
            pltpu.SemaphoreType.DMA((n,)),
            pltpu.SemaphoreType.DMA,
        ],
        compiler_params=pltpu.CompilerParams(
            collective_id=0, has_side_effects=True, vmem_limit_bytes=40 * 1024 * 1024
        ),
        name="sweep_and_send",
    )(warmth, moisture, degree, tally, index, solid_rows)

    chain_after, micro_after, change = pl.pallas_call(
        functools.partial(creep, cap),
        grid=(n // GROUP,),
        out_shape=(
            jax.ShapeDtypeStruct(chain.shape, f32),
            jax.ShapeDtypeStruct(micro.shape, f32),
            jax.ShapeDtypeStruct((n, cp, SITES), f32),
        ),
        in_specs=[
            pl.BlockSpec((GROUP, 2 * cp, SITES), lambda i: (i, 0, 0)),
            pl.BlockSpec((GROUP * cap, KU, SITES), lambda i: (i, 0, 0)),
            pl.BlockSpec((GROUP * cap, SITES), lambda i: (i, 0)),
        ],
        out_specs=(
            pl.BlockSpec((GROUP * cap, KU, SITES), lambda i: (i, 0, 0)),
            pl.BlockSpec((GROUP * cap, SITES), lambda i: (i, 0)),
            pl.BlockSpec((GROUP, cp, SITES), lambda i: (i, 0, 0)),
        ),
        compiler_params=pltpu.CompilerParams(vmem_limit_bytes=40 * 1024 * 1024),
        name="creep",
    )(got, chain, micro)

    creep_cells = pl.pallas_call(
        functools.partial(send_back, n_gz, n_gy),
        out_shape=field,
        in_specs=[vm, sm],
        out_specs=vm,
        scratch_shapes=[
            pltpu.VMEM((n * cp, SITES), f32),
            pltpu.SemaphoreType.DMA((n,)),
            pltpu.SemaphoreType.DMA((n,)),
        ],
        compiler_params=pltpu.CompilerParams(
            collective_id=1, has_side_effects=True, vmem_limit_bytes=40 * 1024 * 1024
        ),
        name="send_back",
    )(change, where)
    return temp, hum, degree_after, creep_cells, chain_after, micro_after


def solution(mesh):
    n_gz, n_gy = mesh.shape["gz"], mesh.shape["gy"]
    cells = P("gz", "gy")
    states = P(("gz", "gy"), None, None)
    tension = P(("gz", "gy"), None)
    return jax.shard_map(
        functools.partial(body, n_gz, n_gy),
        mesh=mesh,
        in_specs=(cells, cells, cells, cells, cells, P(), states, tension),
        out_specs=(cells, cells, cells, cells, states, tension),
        check_vma=False,
    )
```

time: 275 us -> 112 us (0.41)
  waiting for transfers between devices: 104 us -> 0 us
  Pallas kernels: 0 us -> 96.6 us
  local copies, waits for them, and re-layouts: 79.2 us -> 12 us
  starting transfers between devices: 55.6 us -> 0 us
  other arithmetic: 32.7 us -> 1.9 us
    pallas_call x0 -> x3, Pallas kernels: none -> 96.6 us  [the longest x1 62.7 us: body(): pl.pallas_call(functools.partial(sweep_and_send, n_gz, n_gy, cap), out_sh...]
    all_to_all x4 -> x0, waiting for transfers between devices: 96 us -> none  [the longest x1 72.6 us: body(): lax.all_to_all(send_fields, ('gz', 'gy'), split_axis=0, concat_axis=0, ti...]
    scatter x3 -> x0, local copies, waits for them, and re-layouts: 66.2 us -> none  [the longest x1 58 us: body(): jnp.zeros((total_slots, 3, PARCEL_SITES), jnp.float32).at[flat_slot]]
    all_to_all x4 -> x0, starting transfers between devices: 28.7 us -> none  [the longest x1 9.53 us: body(): lax.all_to_all(send_count, ('gz', 'gy'), split_axis=0, concat_axis=0, til...]
    ppermute x12 -> x0, starting transfers between devices: 26.9 us -> none  [the longest x6 19.1 us: with_halo(): lax.ppermute(tail, axis, [(i, (i + 1) % count) for i in range(ends)])]
    select_n x8 -> x0, other arithmetic: 16.3 us -> none  [the longest x1 12.5 us: viscous_strain_advance(): series_result = jnp.where(placed[..., None, :], chain_new, series_prior)]
    unnamed x25 -> x16, local copies, waits for them, and re-layouts: 1.41 us -> 11.5 us
    ppermute x12 -> x0, waiting for transfers between devices: 8.48 us -> none  [the longest x6 8.41 us: with_halo(): lax.ppermute(head, axis, [((i + 1) % count, i) for i in range(ends)])]
  transfers between devices with their start and end apart: 16 -> 0, of which waited for: 4 -> 0; matrix products, arithmetic and copies ran while one was open for 33% -> 0% of each run, Pallas kernels for 0% -> 0%
where the time goes in v1:
time: 112 us; the launch traced here: 111 us
  Pallas kernels  96.6 us (86%)
  local copies, waits for them, and re-layouts  12 us (11%)
  other arithmetic  1.9 us (2%)
    pallas_call x1, Pallas kernels, body(): pl.pallas_call(functools.partial(sweep_and_send, n_gz, n_gy, cap), out_sh...  62.7 us
    pallas_call x1, Pallas kernels, body(): pl.pallas_call(functools.partial(send_back, n_gz, n_gy), out_shape=field,...  27 us
    unnamed x16, local copies, waits for them, and re-layouts  11.5 us
    pallas_call x1, Pallas kernels, body(): pl.pallas_call(functools.partial(creep, cap), grid=(n // GROUP,), out_sha...  6.99 us

profile of v1, /device:TPU:0, one launch (start us, length us, event | category | flops | bytes accessed | tf_op | source)
XLA Modules:
  0.0 111.3 jit_solution(18036098069031768124)
XLA Ops:
  0.6 0.7 sqrt_add_fusion
  1.4 0.1 broadcast.63
  1.4 0.1 reshape.48
  1.6 0.1 broadcast_in_dim.37
  1.6 0.1 broadcast_in_dim.38
  1.7 0.8 copy.18.tally
  2.5 0.8 copy.17
  3.3 0.1 eq.18
  3.4 0.6 select_reduce_fusion
  4.0 0.5 select_reduce_fusion.1
  4.6 0.1 reshape.46
  4.7 0.0 copy-start.2
  4.7 1.0 copy-done.2
  5.7 1.0 copy-done.3
  6.6 1.0 copy-done.4
  7.6 62.7 %sweep_and_send.1 = (f32[48,1536]{1,0:T(8,128)S(1)}, f32[48,1536]{1,0:T(8,128)S(1)}, f32[48,1536]{1,0:T(8,128)S(1)}, f32[32,112,128]{2,1,0:T(8,128)S(1)}) custom-call(f32[48,1536]{1,0:T(8,128)S(1)} %copy-done.2, f32[48,1536]{1,0:T(8,128)S(1)} %copy-done.3, f32[48,1536]{1,0:T(8,128)S(1)} %copy-done.4, s32[48,12]{1,0:T(8,128)S(1)} %copy.18.tally, ...), custom_call_target="tpu_custom_call" | custom-call | tf_op jit(solution)/shard_map/sweep_and_send/pallas_call | solution.py:380
  70.3 3.0 %copy-done = f32[1728,8,128]{2,1,0:T(8,128)S(1)} copy-done((f32[1728,8,128]{2,1,0:T(8,128)S(1)}, f32[1728,8,128]{2,1,0:T(8,128)}, u32[]{:S(2)}) %copy-start) | copy-done | bytes 7077912
  73.3 1.2 %copy-done.1 = f32[1728,128]{1,0:T(8,128)S(1)} copy-done((f32[1728,128]{1,0:T(8,128)S(1)}, f32[1728,128]{1,0:T(8,128)}, u32[]{:S(2)}) %copy-start.1) | copy-done | bytes 884760
  74.5 7.0 %creep.1 = (f32[1728,8,128]{2,1,0:T(8,128)}, f32[1728,128]{1,0:T(8,128)}, f32[32,56,128]{2,1,0:T(8,128)S(1)}) custom-call(f32[32,112,128]{2,1,0:T(8,128)S(1)} %get-tuple-element.16.got, f32[1728,8,128]{2,1,0:T(8,128)S(1)} %copy-done, f32[1728,128]{1,0:T(8,128)S(1)} %copy-done.1), custom_call_target="tpu_custom_call" | custom-call | tf_op jit(solution)/shard_map/creep/pallas_call | solution.py:404
  81.4 27.0 %send_back.1 = f32[48,1536]{1,0:T(8,128)S(1)} custom-call(f32[32,56,128]{2,1,0:T(8,128)S(1)} %get-tuple-element.17.change, s32[576]{0:T(1024)S(1)} %fusion.9.where), custom_call_target="tpu_custom_call" | custom-call | tf_op jit(solution)/shard_map/send_back/pallas_call | solution.py:426
  108.4 0.7 copy.23
  109.1 0.7 copy.24
  109.8 0.7 copy.25
  110.6 0.7 copy.26
  (8 shorter events, 0.1 us)
Async XLA Ops:
  4.7 1.0 copy-start.2
  5.6 1.0 copy-start.3
  6.6 1.0 copy-start.4
  70.3 3.0 %copy-start = (f32[1728,8,128]{2,1,0:T(8,128)S(1)}, f32[1728,8,128]{2,1,0:T(8,128)}, u32[]{:S(2)}) copy-start(f32[1728,8,128]{2,1,0:T(8,128)} %chain.1) | copy-start | bytes 21233668
  73.3 1.2 %copy-start.1 = (f32[1728,128]{1,0:T(8,128)S(1)}, f32[1728,128]{1,0:T(8,128)}, u32[]{:S(2)}) copy-start(f32[1728,128]{1,0:T(8,128)} %micro.1) | copy-start | bytes 2654212

commit v2 on v1

--- a/solution.py
+++ b/solution.py
@@ -15,6 +15,8 @@
 PAD = 128
 TOP = 8
 GROUP = 4
+DIRECT = 24
+SPILL = 40
 DRY = 0.05 + 0.95 / (1.0 + 5.0**16)
 MESH = pl.DeviceIdType.MESH
 
@@ -57,20 +59,38 @@
 
 
 def sweep_and_send(
-    n_gz, n_gy, cap,
-    warmth, moisture, degree, tally, index, solid,
-    temp_out, hum_out, degree_out, got,
-    ext, diff, z_send, z_recv, blocks, send, z_sems, y_sems, out_sems, in_sems, own_sem,
+    n_gz, n_gy, lean,
+    warmth, moisture, degree, tally, index, spill_index, notes,
+    temp_out, hum_out, degree_out, blocks, notes_in, *rest,
 ):
+    if lean:
+        got, got_spill = rest[:2]
+        rest = rest[2:]
+    ext, diff, z_send, z_recv, z_sems, y_sems, note_out, note_in = rest[:8]
+    if lean:
+        send, out_sems, in_sems, own_sems, relay_out, relay_in = rest[8:]
     n = n_gz * n_gy
     rows, cols = warmth.shape
     wide = cols + 2 * PAD
     per_row = cols // SITES
-    cp = padded_rows(cap + 1)
     gz = lax.axis_index("gz")
     gy = lax.axis_index("gy")
     me = gz * n_gy + gy
     greet_all(n, n_gy, me)
+
+    def note_copy(o, at):
+        return pltpu.make_async_remote_copy(
+            src_ref=notes.at[o],
+            dst_ref=notes_in.at[at],
+            send_sem=note_out.at[o],
+            recv_sem=note_in.at[at],
+            device_id=(o // n_gy, lax.rem(o, n_gy)),
+            device_id_type=MESH,
+        )
+
+    def tell(i, carry):
+        note_copy(partner(i, n, me), me).start()
+        return carry
 
     x = lax.rem(lax.broadcasted_iota(jnp.int32, (8, cols), 1), NX)
     has_west = x > 0
@@ -115,6 +135,10 @@
         for side in range(2):
             pl.when(beside[side])(lambda side=side: y_copy(side).start())
             pl.when(there[side])(lambda side=side: z_copy(side).start())
+
+        if s == 0:
+            lax.fori_loop(0, n - 1, tell, 0)
+            notes_in[me] = notes[me]
 
         for side in range(2):
 
@@ -205,33 +229,80 @@
     blocks[0, nb : nb + 8, :] = jnp.zeros((8, SITES), jnp.float32)
     blocks[1, nb : nb + 8, :] = jnp.zeros((8, SITES), jnp.float32)
 
-    def copy_to(i, o):
-        return pltpu.make_async_remote_copy(
-            src_ref=send.at[o],
-            dst_ref=got.at[me],
-            send_sem=out_sems.at[o],
-            recv_sem=in_sems.at[me],
-            device_id=(o // n_gy, lax.rem(o, n_gy)),
-            device_id_type=MESH,
-        )
-
-    def fill(o):
-        for l in range(cap):
-            k = index[o * cap + l]
-            send[o, l : l + 1, :] = blocks[0, pl.ds(k, 1), :]
-            send[o, cp + l : cp + l + 1, :] = blocks[1, pl.ds(k, 1), :]
-        send[o, cap : cap + 1, :] = solid[pl.ds(o, 1), :]
-
-    def push(i, carry):
-        o = partner(i, n, me)
-        fill(o)
-        copy_to(i, o).start()
-        return carry
-
-    lax.fori_loop(0, n - 1, push, 0)
-    fill(me)
-    own_copy = pltpu.make_async_copy(send.at[me], got.at[me], own_sem)
-    own_copy.start()
+    if lean:
+        z, x = gz // 2, lax.rem(gz, 2)
+        y, core = gy // 2, lax.rem(gy, 2)
+        depth = n // 8
+
+        def spill_copy(sem, arrived, base, count, to):
+            part = got_spill.at[pl.ds(base, count)]
+            return pltpu.make_async_remote_copy(
+                src_ref=part,
+                dst_ref=part,
+                send_sem=relay_out.at[sem],
+                recv_sem=relay_in.at[arrived],
+                device_id=to,
+                device_id_type=MESH,
+            )
+
+        line = (core * 4 + x * 2 + y) * depth
+        for l in range(SPILL):
+            k = spill_index[l]
+            got_spill[line + z, l : l + 1, :] = blocks[0, pl.ds(k, 1), :]
+            got_spill[line + z, SPILL + l : SPILL + l + 1, :] = blocks[1, pl.ds(k, 1), :]
+
+        def z_other(d):
+            return lax.rem(z + d, depth)
+
+        for d in range(1, depth):
+            spill_copy(d, depth - d, line + z, 1, (z_other(d) * 2 + x, gy)).start()
+
+        def fill(o):
+            for l in range(DIRECT):
+                k = index[o * DIRECT + l]
+                send[o, l : l + 1, :] = blocks[0, pl.ds(k, 1), :]
+                send[o, DIRECT + l : DIRECT + l + 1, :] = blocks[1, pl.ds(k, 1), :]
+
+        def row_copy(o, at):
+            return pltpu.make_async_remote_copy(
+                src_ref=send.at[o],
+                dst_ref=got.at[at],
+                send_sem=out_sems.at[o],
+                recv_sem=in_sems.at[at],
+                device_id=(o // n_gy, lax.rem(o, n_gy)),
+                device_id_type=MESH,
+            )
+
+        def push(i, carry):
+            o = partner(i, n, me)
+            fill(o)
+            row_copy(o, me).start()
+            return carry
+
+        lax.fori_loop(0, n - 1, push, 0)
+        fill(me)
+        own_copy = pltpu.make_async_copy(send.at[me], got.at[me], own_sems)
+        own_copy.start()
+
+        for d in range(1, depth):
+            spill_copy(d, depth - d, line + z_other(d), 1, (z_other(d) * 2 + x, gy)).wait_recv()
+        spill_copy(depth, depth, line, depth, (gz, (1 - y) * 2 + core)).start()
+        other = (core * 4 + x * 2 + 1 - y) * depth
+        spill_copy(depth, depth, other, depth, (gz, (1 - y) * 2 + core)).wait_recv()
+        pair = (core * 4 + x * 2) * depth
+        spill_copy(depth + 1, depth + 1, pair, 2 * depth, (z * 2 + 1 - x, gy)).start()
+        other = (core * 4 + (1 - x) * 2) * depth
+        spill_copy(depth + 1, depth + 1, other, 2 * depth, (z * 2 + 1 - x, gy)).wait_recv()
+        half = core * 4 * depth
+        spill_copy(depth + 2, depth + 2, half, 4 * depth, (gz, y * 2 + 1 - core)).start()
+        other = (1 - core) * 4 * depth
+        spill_copy(depth + 2, depth + 2, other, 4 * depth, (gz, y * 2 + 1 - core)).wait_recv()
+
+        for d in range(1, depth):
+            spill_copy(d, depth - d, line + z, 1, (z_other(d) * 2 + x, gy)).wait_send()
+        spill_copy(depth, depth, line, depth, (gz, (1 - y) * 2 + core)).wait_send()
+        spill_copy(depth + 1, depth + 1, pair, 2 * depth, (z * 2 + 1 - x, gy)).wait_send()
+        spill_copy(depth + 2, depth + 2, half, 4 * depth, (gz, y * 2 + 1 - core)).wait_send()
 
     for s in range(SWEEPS):
         for side in range(2):
@@ -257,18 +328,64 @@
                 ).wait_send()
             )
 
+    def told(i, carry):
+        o = partner(i, n, me)
+        note_copy(o, o).wait()
+        return carry
+
+    lax.fori_loop(0, n - 1, told, 0)
+
+    if lean:
+        own_copy.wait()
+
+        def finish(i, carry):
+            o = partner(i, n, me)
+            row_copy(o, o).wait()
+            return carry
+
+        lax.fori_loop(0, n - 1, finish, 0)
+
+
+def send_dense(
+    n_gz, n_gy, cap, blocks, index, solid, got, send, out_sems, in_sems, own_sem
+):
+    n = n_gz * n_gy
+    cp = padded_rows(cap + 1)
+    me = lax.axis_index("gz") * n_gy + lax.axis_index("gy")
+    greet_all(n, n_gy, me)
+
+    def row_copy(o, at):
+        return pltpu.make_async_remote_copy(
+            src_ref=send.at[o],
+            dst_ref=got.at[at],
+            send_sem=out_sems.at[o],
+            recv_sem=in_sems.at[at],
+            device_id=(o // n_gy, lax.rem(o, n_gy)),
+            device_id_type=MESH,
+        )
+
+    def fill(o):
+        for l in range(cap):
+            k = index[o * cap + l]
+            send[o, l : l + 1, :] = blocks[0, pl.ds(k, 1), :]
+            send[o, cp + l : cp + l + 1, :] = blocks[1, pl.ds(k, 1), :]
+        send[o, cap : cap + 1, :] = solid[pl.ds(o, 1), :]
+
+    def push(i, carry):
+        o = partner(i, n, me)
+        fill(o)
+        row_copy(o, me).start()
+        return carry
+
+    lax.fori_loop(0, n - 1, push, 0)
+    fill(me)
+    own_copy = pltpu.make_async_copy(send.at[me], got.at[me], own_sem)
+    own_copy.start()
     own_copy.wait()
 
     def finish(i, carry):
         o = partner(i, n, me)
-        pltpu.make_async_remote_copy(
-            src_ref=send.at[o],
-            dst_ref=got.at[o],
-            send_sem=out_sems.at[o],
-            recv_sem=in_sems.at[o],
-            device_id=(o // n_gy, lax.rem(o, n_gy)),
-            device_id_type=MESH,
-        ).wait()
+        row_copy(o, o).wait()
         return carry
 
     lax.fori_loop(0, n - 1, finish, 0)
@@ -303,6 +420,157 @@
         change[q, cap:cp, :] = jnp.zeros((cp - cap, SITES), jnp.float32)
 
 
+def creep_lean(cap, depth, got, spill, notes, chain, micro, chain_out, micro_out, change, change_spill):
+    held = DIRECT + SPILL
+    unit = lax.broadcasted_iota(jnp.int32, (KU, SITES), 0)
+    speed = jnp.full((KU, SITES), -10.0, jnp.float32)
+    for m in range(1, KU):
+        speed = jnp.where(unit == m, -10.0 / 3.0**m, speed)
+    sub = lax.broadcasted_iota(jnp.int32, (cap, SITES), 0)
+    lane = lax.broadcasted_iota(jnp.int32, (cap, SITES), 1)
+    row_id = lax.broadcasted_iota(jnp.int32, (cap, held), 1).astype(jnp.float32)
+    exact = lax.Precision.HIGHEST
+    for q in range(GROUP):
+        base = q * cap
+        source = pl.program_id(0) * GROUP + q
+        z, x = source // 8, lax.rem(source, 8) // 4
+        y, core = lax.rem(source, 4) // 2, lax.rem(source, 2)
+        place = (core * 4 + x * 2 + y) * depth + z
+
+        def column(r):
+            row = notes[q, r : r + 1, :]
+            return jnp.sum(jnp.where(sub == lane, row, 0.0), axis=1, keepdims=True)
+
+        pick = (column(0) == row_id).astype(jnp.float32)
+        solid = column(1)
+        rows_phi = jnp.concatenate([got[q, 0:DIRECT, :], spill[place, 0:SPILL, :]], axis=0)
+        rows_stress = jnp.concatenate(
+            [got[q, DIRECT : 2 * DIRECT, :], spill[place, SPILL : 2 * SPILL, :]], axis=0
+        )
+        both = jnp.concatenate([rows_phi, rows_stress], axis=1)
+        both = jnp.dot(pick, both, precision=exact, preferred_element_type=jnp.float32)
+        phi = both[:, :SITES]
+        stress = both[:, SITES:]
+        s0 = micro[base : base + cap, :]
+        s1 = s0 / (1.0 + 0.2 * phi * s0)
+        micro_out[base : base + cap, :] = s1
+        flow = 0.1 * phi * s1 * stress
+        parts = []
+        for l0 in range(0, cap, 8):
+            l1 = min(l0 + 8, cap)
+            old = chain[base + l0 : base + l1]
+            decay = jnp.exp(phi[l0:l1][:, None, :] * speed[None])
+            new = decay * old + 0.15 * (1.0 - decay) * stress[l0:l1][:, None, :]
+            chain_out[base + l0 : base + l1] = new
+            kelvin = jnp.sum(new - old, axis=1)
+            parts.append(solid[l0:l1] * kelvin + flow[l0:l1])
+        slots = jnp.concatenate(parts, axis=0)
+        result = lax.dot_general(
+            pick, slots, (((0,), (0,)), ((), ())),
+            precision=exact, preferred_element_type=jnp.float32,
+        )
+        change[q] = result[:DIRECT]
+        change_spill[place] = result[DIRECT:]
+
+
+def send_back_lean(
+    n_gz, n_gy, change, spill, where, out,
+    back, tmp, half, pair, line, ends, out_sems, in_sems, relay_out, relay_in,
+):
+    n = n_gz * n_gy
+    rows, cols = out.shape
+    depth = n // 8
+    gz = lax.axis_index("gz")
+    gy = lax.axis_index("gy")
+    me = gz * n_gy + gy
+    z, x = gz // 2, lax.rem(gz, 2)
+    y, core = gy // 2, lax.rem(gy, 2)
+    greet_all(n, n_gy, me)
+
+    def relay(src, dst, sem, arrived, to):
+        return pltpu.make_async_remote_copy(
+            src_ref=src, dst_ref=dst,
+            send_sem=relay_out.at[sem], recv_sem=relay_in.at[arrived],
+            device_id=to, device_id_type=MESH,
+        )
+
+    across = relay(
+        spill.at[pl.ds((1 - core) * 4 * depth, 4 * depth)],
+        tmp.at[pl.ds(0, 4 * depth)], depth + 2, depth + 2, (gz, y * 2 + 1 - core),
+    )
+    across.start()
+
+    def row_copy(o, at):
+        return pltpu.make_async_remote_copy(
+            src_ref=change.at[o],
+            dst_ref=back.at[pl.ds(pl.multiple_of(at * DIRECT, 8), DIRECT)],
+            send_sem=out_sems.at[o],
+            recv_sem=in_sems.at[at],
+            device_id=(o // n_gy, lax.rem(o, n_gy)),
+            device_id_type=MESH,
+        )
+
+    def push(i, carry):
+        row_copy(partner(i, n, me), me).start()
+        return carry
+
+    lax.fori_loop(0, n - 1, push, 0)
+    back[pl.ds(pl.multiple_of(me * DIRECT, 8), DIRECT), :] = change[me]
+
+    across.wait_recv()
+    half[...] = spill[pl.ds(core * 4 * depth, 4 * depth)] + tmp[0 : 4 * depth]
+    along = relay(
+        half.at[pl.ds((1 - x) * 2 * depth, 2 * depth)],
+        tmp.at[pl.ds(4 * depth, 2 * depth)], depth + 1, depth + 1, (z * 2 + 1 - x, gy),
+    )
+    along.start()
+    along.wait_recv()
+    pair[...] = half[pl.ds(x * 2 * depth, 2 * depth)] + tmp[4 * depth : 6 * depth]
+    beside = relay(
+        pair.at[pl.ds((1 - y) * depth, depth)],
+        tmp.at[pl.ds(6 * depth, depth)], depth, depth, (gz, (1 - y) * 2 + core),
+    )
+    beside.start()
+    beside.wait_recv()
+    line[...] = pair[pl.ds(y * depth, depth)] + tmp[6 * depth : 7 * depth]
+
+    def end_copy(d):
+        to = lax.rem(z + d, depth)
+        return relay(line.at[to], ends.at[depth - d], d, depth - d, (to * 2 + x, gy))
+
+    for d in range(1, depth):
+        end_copy(d).start()
+    total = line[z]
+    for d in range(1, depth):
+        end_copy(d).wait_recv()
+    for d in range(1, depth):
+        total = total + ends[d]
+    back[n * DIRECT : n * DIRECT + SPILL, :] = total
+
+    across.wait_send()
+    along.wait_send()
+    beside.wait_send()
+    for d in range(1, depth):
+        end_copy(d).wait_send()
+
+    def finish(i, carry):
+        o = partner(i, n, me)
+        row_copy(o, o).wait()
+        return carry
+
+    lax.fori_loop(0, n - 1, finish, 0)
+    per_row = cols // SITES
+
+    def place(g, carry):
+        r = pl.multiple_of(g * 8, 8)
+        for j in range(per_row):
+            lines = [back[pl.ds(where[(r + k) * per_row + j], 1), :] for k in range(8)]
+            out[pl.ds(r, 8), j * SITES : (j + 1) * SITES] = jnp.concatenate(lines, axis=0)
+        return carry
+
+    lax.fori_loop(0, rows // 8, place, 0)
+
+
 def send_back(n_gz, n_gy, change, where, out, back, out_sems, in_sems):
     n = n_gz * n_gy
     rows, cols = out.shape
@@ -368,76 +636,186 @@
     age = 2400.0 - jnp.repeat(local_times, LIFT).astype(f32)
     solid = jnp.sqrt(600.0 / age) + 0.2
     flat = keeper.reshape(-1)
-    hit = flat[None, :] == jnp.arange(slots, dtype=jnp.int32)[:, None]
+    slot_id = jnp.arange(slots, dtype=jnp.int32)
+    hit = flat[None, :] == slot_id[:, None]
     block = jnp.arange(nb, dtype=jnp.int32)
     held = (block % per_row) * rows + block // per_row
-    index = nb + jnp.sum(jnp.where(hit, held[None, :] - nb, 0), axis=1)
     solid_slot = jnp.sum(jnp.where(hit, jnp.repeat(solid, per_row)[None, :], 0.0), axis=1)
     solid_rows = jnp.pad(solid_slot.reshape(n, cap), ((0, 0), (0, SITES - cap)))
-    where = (flat // cap) * cp + flat % cap
+    lean = cap >= DIRECT + 8 and n % 8 == 0 and n_gy == 4
+    owner = flat // cap
+    earlier = flat[None, :] < flat[:, None]
+    if lean:
+        rank = jnp.sum(earlier & (owner[None, :] == owner[:, None]), axis=1, dtype=jnp.int32)
+        over = rank >= DIRECT
+        spot = jnp.sum(earlier & over[None, :], axis=1, dtype=jnp.int32)
+        spilled = jnp.sum(over, dtype=jnp.int32)
+        code = jnp.where(over, DIRECT + spot, rank)
+        slot_map = jnp.sum(jnp.where(hit, code[None, :] + 1, 0), axis=1) - 1
+        target = jnp.where(over, n * DIRECT + spot, owner * DIRECT + rank)
+        line_id = jnp.arange(n * DIRECT + SPILL, dtype=jnp.int32)
+        fits = target[None, :] == line_id[:, None]
+        index = nb + jnp.sum(jnp.where(fits, held[None, :] - nb, 0), axis=1)
+        index, spill_index = index[: n * DIRECT], index[n * DIRECT :]
+        slot_map = jnp.pad(slot_map.reshape(n, cap).astype(f32), ((0, 0), (0, SITES - cap)))
+        count = jnp.broadcast_to(spilled.astype(f32), (n, SITES))
+        where_back = jnp.minimum(target, n * DIRECT + SPILL - 1)
+        notes = [slot_map, solid_rows, count]
+    else:
+        index = spill_index = jnp.zeros((8,), jnp.int32)
+        notes = [solid_rows, solid_rows, solid_rows]
+    notes = jnp.stack(notes + [jnp.zeros((n, SITES), f32)] * 5, axis=1)
 
     field = jax.ShapeDtypeStruct((rows, cols), f32)
-    temp, hum, degree_after, got = pl.pallas_call(
-        functools.partial(sweep_and_send, n_gz, n_gy, cap),
-        out_shape=(field, field, field, jax.ShapeDtypeStruct((n, 2 * cp, SITES), f32)),
-        in_specs=[vm, vm, vm, vm, sm, vm],
-        out_specs=(vm, vm, vm, hbm),
-        scratch_shapes=[
-            pltpu.VMEM((SWEEPS, 2, rows + 2 * TOP, cols + 2 * PAD), f32),
-            pltpu.VMEM((rows + 2 * TOP, cols + 2 * PAD), f32),
-            pltpu.VMEM((SWEEPS, 2, 2, cols), f32),
-            pltpu.VMEM((SWEEPS, 2, 2, cols), f32),
-            pltpu.VMEM((2, nb + 8, SITES), f32),
-            pltpu.VMEM((n, 2 * cp, SITES), f32),
-            pltpu.SemaphoreType.DMA((SWEEPS, 2, 2)),
-            pltpu.SemaphoreType.DMA((SWEEPS, 2, 2)),
+    outs = [field, field, field, jax.ShapeDtypeStruct((2, nb + 8, SITES), f32)]
+    outs += [jax.ShapeDtypeStruct((n, 8, SITES), f32)]
+    scratch = [
+        pltpu.VMEM((SWEEPS, 2, rows + 2 * TOP, cols + 2 * PAD), f32),
+        pltpu.VMEM((rows + 2 * TOP, cols + 2 * PAD), f32),
+        pltpu.VMEM((SWEEPS, 2, 2, cols), f32),
+        pltpu.VMEM((SWEEPS, 2, 2, cols), f32),
+        pltpu.SemaphoreType.DMA((SWEEPS, 2, 2)),
+        pltpu.SemaphoreType.DMA((SWEEPS, 2, 2)),
+        pltpu.SemaphoreType.DMA((n,)),
+        pltpu.SemaphoreType.DMA((n,)),
+    ]
+    out_specs = [vm] * 5
+    if lean:
+        outs += [jax.ShapeDtypeStruct((n, 2 * DIRECT, SITES), f32)]
+        outs += [jax.ShapeDtypeStruct((n, 2 * SPILL, SITES), f32)]
+        out_specs += [hbm, vm]
+        scratch += [
+            pltpu.VMEM((n, 2 * DIRECT, SITES), f32),
             pltpu.SemaphoreType.DMA((n,)),
             pltpu.SemaphoreType.DMA((n,)),
             pltpu.SemaphoreType.DMA,
-        ],
+            pltpu.SemaphoreType.DMA((n // 8 + 3,)),
+            pltpu.SemaphoreType.DMA((n // 8 + 3,)),
+        ]
+    limit = 40 * 1024 * 1024
+    results = pl.pallas_call(
+        functools.partial(sweep_and_send, n_gz, n_gy, lean),
+        out_shape=tuple(outs),
+        in_specs=[vm, vm, vm, vm, sm, sm, vm],
+        out_specs=tuple(out_specs),
+        scratch_shapes=scratch,
         compiler_params=pltpu.CompilerParams(
-            collective_id=0, has_side_effects=True, vmem_limit_bytes=40 * 1024 * 1024
+            collective_id=0, has_side_effects=True, vmem_limit_bytes=limit
         ),
         name="sweep_and_send",
-    )(warmth, moisture, degree, tally, index, solid_rows)
-
-    chain_after, micro_after, change = pl.pallas_call(
-        functools.partial(creep, cap),
-        grid=(n // GROUP,),
-        out_shape=(
-            jax.ShapeDtypeStruct(chain.shape, f32),
-            jax.ShapeDtypeStruct(micro.shape, f32),
-            jax.ShapeDtypeStruct((n, cp, SITES), f32),
-        ),
-        in_specs=[
-            pl.BlockSpec((GROUP, 2 * cp, SITES), lambda i: (i, 0, 0)),
-            pl.BlockSpec((GROUP * cap, KU, SITES), lambda i: (i, 0, 0)),
-            pl.BlockSpec((GROUP * cap, SITES), lambda i: (i, 0)),
-        ],
-        out_specs=(
-            pl.BlockSpec((GROUP * cap, KU, SITES), lambda i: (i, 0, 0)),
-            pl.BlockSpec((GROUP * cap, SITES), lambda i: (i, 0)),
-            pl.BlockSpec((GROUP, cp, SITES), lambda i: (i, 0, 0)),
-        ),
-        compiler_params=pltpu.CompilerParams(vmem_limit_bytes=40 * 1024 * 1024),
-        name="creep",
-    )(got, chain, micro)
-
-    creep_cells = pl.pallas_call(
-        functools.partial(send_back, n_gz, n_gy),
-        out_shape=field,
-        in_specs=[vm, sm],
-        out_specs=vm,
-        scratch_shapes=[
-            pltpu.VMEM((n * cp, SITES), f32),
-            pltpu.SemaphoreType.DMA((n,)),
-            pltpu.SemaphoreType.DMA((n,)),
-        ],
-        compiler_params=pltpu.CompilerParams(
-            collective_id=1, has_side_effects=True, vmem_limit_bytes=40 * 1024 * 1024
-        ),
-        name="send_back",
-    )(change, where)
+    )(warmth, moisture, degree, tally, index, spill_index, notes)
+    temp, hum, degree_after, blocks, notes_in = results[:5]
+
+    state_specs = (
+        pl.BlockSpec((GROUP * cap, KU, SITES), lambda i: (i, 0, 0)),
+        pl.BlockSpec((GROUP * cap, SITES), lambda i: (i, 0)),
+    )
+    state_shapes = (
+        jax.ShapeDtypeStruct(chain.shape, f32),
+        jax.ShapeDtypeStruct(micro.shape, f32),
+    )
+
+    def dense_tail(*_):
+        index = nb + jnp.sum(jnp.where(hit, held[None, :] - nb, 0), axis=1)
+        where = (flat // cap) * cp + flat % cap
+        got = pl.pallas_call(
+            functools.partial(send_dense, n_gz, n_gy, cap),
+            out_shape=jax.ShapeDtypeStruct((n, 2 * cp, SITES), f32),
+            in_specs=[vm, sm, vm],
+            out_specs=hbm,
+            scratch_shapes=[
+                pltpu.VMEM((n, 2 * cp, SITES), f32),
+                pltpu.SemaphoreType.DMA((n,)),
+                pltpu.SemaphoreType.DMA((n,)),
+                pltpu.SemaphoreType.DMA,
+            ],
+            compiler_params=pltpu.CompilerParams(
+                collective_id=2, has_side_effects=True, vmem_limit_bytes=limit
+            ),
+            name="send_dense",
+        )(blocks, index, solid_rows)
+        chain_after, micro_after, change = pl.pallas_call(
+            functools.partial(creep, cap),
+            grid=(n // GROUP,),
+            out_shape=state_shapes + (jax.ShapeDtypeStruct((n, cp, SITES), f32),),
+            in_specs=[pl.BlockSpec((GROUP, 2 * cp, SITES), lambda i: (i, 0, 0)), *state_specs],
+            out_specs=(*state_specs, pl.BlockSpec((GROUP, cp, SITES), lambda i: (i, 0, 0))),
+            compiler_params=pltpu.CompilerParams(vmem_limit_bytes=limit),
+            name="creep",
+        )(got, chain, micro)
+        cells = pl.pallas_call(
+            functools.partial(send_back, n_gz, n_gy),
+            out_shape=field,
+            in_specs=[vm, sm],
+            out_specs=vm,
+            scratch_shapes=[
+                pltpu.VMEM((n * cp, SITES), f32),
+                pltpu.SemaphoreType.DMA((n,)),
+                pltpu.SemaphoreType.DMA((n,)),
+            ],
+            compiler_params=pltpu.CompilerParams(
+                collective_id=1, has_side_effects=True, vmem_limit_bytes=limit
+            ),
+            name="send_back",
+        )(change, where)
+        return cells, chain_after, micro_after
+
+    def lean_tail(got, got_spill):
+        depth = n // 8
+        whole = pl.BlockSpec((n, SPILL, SITES), lambda i: (0, 0, 0))
+        chain_after, micro_after, change, change_spill = pl.pallas_call(
+            functools.partial(creep_lean, cap, depth),
+            grid=(n // GROUP,),
+            out_shape=state_shapes
+            + (
+                jax.ShapeDtypeStruct((n, DIRECT, SITES), f32),
+                jax.ShapeDtypeStruct((n, SPILL, SITES), f32),
+            ),
+            in_specs=[
+                pl.BlockSpec((GROUP, 2 * DIRECT, SITES), lambda i: (i, 0, 0)),
+                pl.BlockSpec((n, 2 * SPILL, SITES), lambda i: (0, 0, 0)),
+                pl.BlockSpec((GROUP, 8, SITES), lambda i: (i, 0, 0)),
+                *state_specs,
+            ],
+            out_specs=(
+                *state_specs,
+                pl.BlockSpec((GROUP, DIRECT, SITES), lambda i: (i, 0, 0)),
+                whole,
+            ),
+            compiler_params=pltpu.CompilerParams(vmem_limit_bytes=limit),
+            name="creep_lean",
+        )(got, got_spill, notes_in, chain, micro)
+        cells = pl.pallas_call(
+            functools.partial(send_back_lean, n_gz, n_gy),
+            out_shape=field,
+            in_specs=[vm, vm, sm],
+            out_specs=vm,
+            scratch_shapes=[
+                pltpu.VMEM((n * DIRECT + SPILL, SITES), f32),
+                pltpu.VMEM((7 * depth, SPILL, SITES), f32),
+                pltpu.VMEM((4 * depth, SPILL, SITES), f32),
+                pltpu.VMEM((2 * depth, SPILL, SITES), f32),
+                pltpu.VMEM((depth, SPILL, SITES), f32),
+                pltpu.VMEM((depth, SPILL, SITES), f32),
+                pltpu.SemaphoreType.DMA((n,)),
+                pltpu.SemaphoreType.DMA((n,)),
+                pltpu.SemaphoreType.DMA((depth + 3,)),
+                pltpu.SemaphoreType.DMA((depth + 3,)),
+            ],
+            compiler_params=pltpu.CompilerParams(
+                collective_id=3, has_side_effects=True, vmem_limit_bytes=limit
+            ),
+            name="send_back_lean",
+        )(change, change_spill, where_back)
+        return cells, chain_after, micro_after
+
+    if lean:
+        fits_all = jnp.max(notes_in[:, 2, 0]) <= SPILL
+        creep_cells, chain_after, micro_after = lax.cond(
+            fits_all, lean_tail, dense_tail, *results[5:]
+        )
+    else:
+        creep_cells, chain_after, micro_after = dense_tail()
     return temp, hum, degree_after, creep_cells, chain_after, micro_after
 
 

time: 112 us -> 103 us (0.920)
  Pallas kernels: 96.6 us -> 89.6 us
  local copies, waits for them, and re-layouts: 12 us -> 5.25 us
  other arithmetic: 1.9 us -> 5.24 us
  between operations: 0.74 us -> 2.17 us
    pallas_call x3, Pallas kernels: 96.6 us -> 89.6 us  [the longest x1 46 us: body(): pl.pallas_call(functools.partial(sweep_and_send, n_gz, n_gy, lean), out_s...]
    unnamed x16 -> x12, local copies, waits for them, and re-layouts: 11.5 us -> 4.43 us
    reduce_sum x1 -> x5, other arithmetic: 0.53 us -> 2.27 us  [the longest x1 0.64 us: body(): spilled = jnp.sum(over, dtype=jnp.int32)]
where the time goes in v2:
time: 103 us; the launch traced here: 102 us
  Pallas kernels  89.6 us (87%)
  local copies, waits for them, and re-layouts  5.25 us (5%)
  other arithmetic  5.24 us (5%)
  between operations  2.17 us (2%)
    pallas_call x1, Pallas kernels, body(): pl.pallas_call(functools.partial(sweep_and_send, n_gz, n_gy, lean), out_s...  46 us
    pallas_call x1, Pallas kernels, lean_tail(): pl.pallas_call(functools.partial(send_back_lean, n_gz, n_gy), out_shape=f...  27.8 us
    pallas_call x1, Pallas kernels, lean_tail(): pl.pallas_call(functools.partial(creep_lean, cap, depth), grid=(n // GROU...  15.8 us
    unnamed x12, local copies, waits for them, and re-layouts  4.43 us

profile of v2, /device:TPU:0, one launch (start us, length us, event | category | flops | bytes accessed | tf_op | source)
XLA Modules:
  0.0 102.3 jit_solution(17708608406951588755)
XLA Ops:
  0.7 0.8 sqrt_add_fusion
  1.7 0.1 broadcast_in_dim.69
  1.8 0.8 copy.18.tally
  2.6 0.8 copy.17
  3.4 0.1 lt.30
  3.5 0.6 select_reduce_fusion.1
  4.1 0.4 convert_reduce_fusion.1
  4.5 0.6 convert_reduce_fusion.2
  5.8 0.4 convert_reduce_fusion
  6.2 0.1 reshape.116
  6.3 0.6 select_reduce_fusion.2
  6.9 0.3 select_reduce_fusion.3
  7.2 0.1 convert_element_type.32
  7.4 0.1 stack.15.notes
  7.5 0.9 iota_compare_fusion
  8.4 46.0 %sweep_and_send.1 = (f32[48,1536]{1,0:T(8,128)S(1)}, f32[48,1536]{1,0:T(8,128)S(1)}, f32[48,1536]{1,0:T(8,128)S(1)}, f32[2,584,128]{2,1,0:T(8,128)}, f32[32,8,12...) custom-call(f32[48,1536]{1,0:T(8,128)S(1)} %copy-done, f32[48,1536]{1,0:T(8,128)S(1)} %copy-done.1, ...), custom_call_target="tpu_custom_call" | custom-call | tf_op jit(solution)/shard_map/sweep_and_send/pallas_call | solution.py:696
  54.4 0.6 slice_reduce_fusion
  55.8 43.6 %conditional.1 = (f32[48,1536]{1,0:T(8,128)S(1)}, f32[1728,8,128]{2,1,0:T(8,128)}, f32[1728,128]{1,0:T(8,128)}) conditional(s32[]{:T(128)} %convert_element_type.36, (s32[576]{0:T(1024)S(1)}, s32[576]{0:T(1024)S(1)}, pred[576]{0:T(1024)(128)(4,1)S(1)}, s32[576]{0:T(1024)S(1)}, s32[576]{0:T(1024)S(1)}, /*index=5*/s32[576]{0:T(1024)S(1)}, ...), branch_computations={%region_7.9_spmd, %region_9.10_spmd} | conditional | flops 2005632 | bytes 4580980 | solution.py:814
  55.8 15.8 %creep_lean.2 = (f32[1728,8,128]{2,1,0:T(8,128)}, f32[1728,128]{1,0:T(8,128)}, f32[32,24,128]{2,1,0:T(8,128)S(1)}, f32[32,40,128]{2,1,0:T(8,128)S(1)}) custom-call(f32[32,48,128]{2,1,0:T(8,128)} %get-tuple-element.174.got, f32[32,80,128]{2,1,0:T(8,128)} %get-tuple-element.175.spill, f32[32,8,128]{2,1,0:T(8,128)S(1)} %get-tuple-element.176.notes, ...), custom_call_target="tpu_custom_call" | custom-call | tf_op jit(solution)/shard_map/cond/branch_1_fun/creep_lean/pallas_call | solution.py:766
  71.6 27.8 %send_back_lean.2 = f32[48,1536]{1,0:T(8,128)S(1)} custom-call(f32[32,24,128]{2,1,0:T(8,128)S(1)} %get-tuple-element.179.change, f32[32,40,128]{2,1,0:T(8,128)S(1)} %get-tuple-element.180.spill, s32[576]{0:T(1024)S(1)} %fusion.10.where), custom_call_target="tpu_custom_call" | custom-call | tf_op jit(solution)/shard_map/cond/branch_1_fun/send_back_lean/pallas_call | solution.py:788
  99.4 0.7 copy.29
  100.1 0.7 copy.30
  100.8 0.7 copy.31
  101.5 0.7 copy.32
  (28 shorter events, 0.4 us)
Async XLA Ops:
  0.6 7.8 %copy-start.2 = (f32[48,1536]{1,0:T(8,128)S(1)}, f32[48,1536]{1,0:T(8,128)}, u32[]{:S(2)}) copy-start(f32[48,1536]{1,0:T(8,128)} %degree.1) | copy-start | bytes 884740
  0.6 7.8 %copy-start.1 = (f32[48,1536]{1,0:T(8,128)S(1)}, f32[48,1536]{1,0:T(8,128)}, u32[]{:S(2)}) copy-start(f32[48,1536]{1,0:T(8,128)} %moisture.1) | copy-start | bytes 884740
  0.7 7.8 %copy-start = (f32[48,1536]{1,0:T(8,128)S(1)}, f32[48,1536]{1,0:T(8,128)}, u32[]{:S(2)}) copy-start(f32[48,1536]{1,0:T(8,128)} %warmth.1) | copy-start | bytes 884740

commit v3 on v2

--- a/solution.py
+++ b/solution.py
@@ -420,138 +420,114 @@
         change[q, cap:cp, :] = jnp.zeros((cp - cap, SITES), jnp.float32)
 
 
-def creep_lean(cap, depth, got, spill, notes, chain, micro, chain_out, micro_out, change, change_spill):
+def creep_and_return(
+    n_gz, n_gy, cap,
+    got, spill, notes, micro, where, chain,
+    out, micro_out, chain_out,
+    old_state, new_state, change, back, read_sems, write_sems, out_sems, in_sems,
+):
+    n = n_gz * n_gy
+    depth = n // 8
+    rows, cols = out.shape
+    gz = lax.axis_index("gz")
+    gy = lax.axis_index("gy")
+    me = gz * n_gy + gy
     held = DIRECT + SPILL
+    part = n_gy * cap
+
+    def read(g):
+        at = pl.ds(g * part, part)
+        return pltpu.make_async_copy(chain.at[at], old_state.at[at], read_sems.at[g])
+
+    def write(g):
+        at = pl.ds(g * part, part)
+        return pltpu.make_async_copy(new_state.at[at], chain_out.at[at], write_sems.at[g])
+
+    def turn(i):
+        return lax.rem(gz + n_gz // 2 + i, n_gz)
+
+    def begin(i, carry):
+        read(turn(i)).start()
+        return carry
+
+    lax.fori_loop(0, n_gz, begin, 0)
+    greet_all(n, n_gy, me)
+
     unit = lax.broadcasted_iota(jnp.int32, (KU, SITES), 0)
     speed = jnp.full((KU, SITES), -10.0, jnp.float32)
     for m in range(1, KU):
         speed = jnp.where(unit == m, -10.0 / 3.0**m, speed)
-    sub = lax.broadcasted_iota(jnp.int32, (cap, SITES), 0)
-    lane = lax.broadcasted_iota(jnp.int32, (cap, SITES), 1)
-    row_id = lax.broadcasted_iota(jnp.int32, (cap, held), 1).astype(jnp.float32)
-    exact = lax.Precision.HIGHEST
-    for q in range(GROUP):
-        base = q * cap
-        source = pl.program_id(0) * GROUP + q
-        z, x = source // 8, lax.rem(source, 8) // 4
-        y, core = lax.rem(source, 4) // 2, lax.rem(source, 2)
-        place = (core * 4 + x * 2 + y) * depth + z
-
-        def column(r):
-            row = notes[q, r : r + 1, :]
-            return jnp.sum(jnp.where(sub == lane, row, 0.0), axis=1, keepdims=True)
-
-        pick = (column(0) == row_id).astype(jnp.float32)
-        solid = column(1)
-        rows_phi = jnp.concatenate([got[q, 0:DIRECT, :], spill[place, 0:SPILL, :]], axis=0)
-        rows_stress = jnp.concatenate(
-            [got[q, DIRECT : 2 * DIRECT, :], spill[place, SPILL : 2 * SPILL, :]], axis=0
-        )
-        both = jnp.concatenate([rows_phi, rows_stress], axis=1)
-        both = jnp.dot(pick, both, precision=exact, preferred_element_type=jnp.float32)
-        phi = both[:, :SITES]
-        stress = both[:, SITES:]
-        s0 = micro[base : base + cap, :]
-        s1 = s0 / (1.0 + 0.2 * phi * s0)
-        micro_out[base : base + cap, :] = s1
-        flow = 0.1 * phi * s1 * stress
-        parts = []
-        for l0 in range(0, cap, 8):
-            l1 = min(l0 + 8, cap)
-            old = chain[base + l0 : base + l1]
-            decay = jnp.exp(phi[l0:l1][:, None, :] * speed[None])
-            new = decay * old + 0.15 * (1.0 - decay) * stress[l0:l1][:, None, :]
-            chain_out[base + l0 : base + l1] = new
-            kelvin = jnp.sum(new - old, axis=1)
-            parts.append(solid[l0:l1] * kelvin + flow[l0:l1])
-        slots = jnp.concatenate(parts, axis=0)
-        result = lax.dot_general(
-            pick, slots, (((0,), (0,)), ((), ())),
-            precision=exact, preferred_element_type=jnp.float32,
-        )
-        change[q] = result[:DIRECT]
-        change_spill[place] = result[DIRECT:]
-
-
-def send_back_lean(
-    n_gz, n_gy, change, spill, where, out,
-    back, tmp, half, pair, line, ends, out_sems, in_sems, relay_out, relay_in,
-):
-    n = n_gz * n_gy
-    rows, cols = out.shape
-    depth = n // 8
-    gz = lax.axis_index("gz")
-    gy = lax.axis_index("gy")
-    me = gz * n_gy + gy
-    z, x = gz // 2, lax.rem(gz, 2)
-    y, core = gy // 2, lax.rem(gy, 2)
-    greet_all(n, n_gy, me)
-
-    def relay(src, dst, sem, arrived, to):
-        return pltpu.make_async_remote_copy(
-            src_ref=src, dst_ref=dst,
-            send_sem=relay_out.at[sem], recv_sem=relay_in.at[arrived],
-            device_id=to, device_id_type=MESH,
-        )
-
-    across = relay(
-        spill.at[pl.ds((1 - core) * 4 * depth, 4 * depth)],
-        tmp.at[pl.ds(0, 4 * depth)], depth + 2, depth + 2, (gz, y * 2 + 1 - core),
-    )
-    across.start()
+    tall = -(-cap // 16) * 16
+    sub = lax.broadcasted_iota(jnp.int32, (tall, SITES), 0)
+    lane = lax.broadcasted_iota(jnp.int32, (tall, SITES), 1)
+    row_id = lax.rem(lax.broadcasted_iota(jnp.int32, (tall, 3 * held), 1), held)
+    row_id = row_id.astype(jnp.float32)
 
     def row_copy(o, at):
         return pltpu.make_async_remote_copy(
             src_ref=change.at[o],
-            dst_ref=back.at[pl.ds(pl.multiple_of(at * DIRECT, 8), DIRECT)],
+            dst_ref=back.at[at],
             send_sem=out_sems.at[o],
             recv_sem=in_sems.at[at],
             device_id=(o // n_gy, lax.rem(o, n_gy)),
             device_id_type=MESH,
         )
 
-    def push(i, carry):
-        row_copy(partner(i, n, me), me).start()
-        return carry
-
-    lax.fori_loop(0, n - 1, push, 0)
-    back[pl.ds(pl.multiple_of(me * DIRECT, 8), DIRECT), :] = change[me]
-
-    across.wait_recv()
-    half[...] = spill[pl.ds(core * 4 * depth, 4 * depth)] + tmp[0 : 4 * depth]
-    along = relay(
-        half.at[pl.ds((1 - x) * 2 * depth, 2 * depth)],
-        tmp.at[pl.ds(4 * depth, 2 * depth)], depth + 1, depth + 1, (z * 2 + 1 - x, gy),
-    )
-    along.start()
-    along.wait_recv()
-    pair[...] = half[pl.ds(x * 2 * depth, 2 * depth)] + tmp[4 * depth : 6 * depth]
-    beside = relay(
-        pair.at[pl.ds((1 - y) * depth, depth)],
-        tmp.at[pl.ds(6 * depth, depth)], depth, depth, (gz, (1 - y) * 2 + core),
-    )
-    beside.start()
-    beside.wait_recv()
-    line[...] = pair[pl.ds(y * depth, depth)] + tmp[6 * depth : 7 * depth]
-
-    def end_copy(d):
-        to = lax.rem(z + d, depth)
-        return relay(line.at[to], ends.at[depth - d], d, depth - d, (to * 2 + x, gy))
-
-    for d in range(1, depth):
-        end_copy(d).start()
-    total = line[z]
-    for d in range(1, depth):
-        end_copy(d).wait_recv()
-    for d in range(1, depth):
-        total = total + ends[d]
-    back[n * DIRECT : n * DIRECT + SPILL, :] = total
-
-    across.wait_send()
-    along.wait_send()
-    beside.wait_send()
-    for d in range(1, depth):
-        end_copy(d).wait_send()
+    def group(i, carry):
+        g = turn(i)
+        read(g).wait()
+        start = pl.multiple_of(g * part, 8)
+        s0 = micro[pl.ds(start, part), :]
+        z, x = g // 2, lax.rem(g, 2)
+        all_phi = []
+        all_stress = []
+        all_solid = []
+        for q in range(n_gy):
+            o = g * n_gy + q
+            place = (q % 2 * 4 + x * 2 + q // 2) * depth + z
+
+            def column(r):
+                row = notes[o, r : r + 1, :]
+                return jnp.sum(jnp.where(sub == lane, row, 0.0), axis=1, keepdims=True)
+
+            pick = jnp.where(column(0) == row_id, 1.0, 0.0).astype(jnp.bfloat16)
+            all_solid.append(column(1)[:cap])
+            rows_phi = jnp.concatenate([got[o, 0:DIRECT, :], spill[place, 0:SPILL, :]], axis=0)
+            rows_stress = jnp.concatenate(
+                [got[o, DIRECT : 2 * DIRECT, :], spill[place, SPILL : 2 * SPILL, :]], axis=0
+            )
+            both = jnp.concatenate([rows_phi, rows_stress], axis=1)
+            high = both.astype(jnp.bfloat16)
+            left = both - high.astype(jnp.float32)
+            middle = left.astype(jnp.bfloat16)
+            low = (left - middle.astype(jnp.float32)).astype(jnp.bfloat16)
+            parts = jnp.concatenate([high, middle, low], axis=0)
+            both = jnp.dot(pick, parts, preferred_element_type=jnp.float32)
+            all_phi.append(both[:cap, :SITES])
+            all_stress.append(both[:cap, SITES:])
+        phis = jnp.concatenate(all_phi, axis=0)
+        s1 = s0 / (1.0 + 0.2 * phis * s0)
+        micro_out[pl.ds(start, part), :] = s1
+        for q in range(n_gy):
+            o = g * n_gy + q
+            phi, stress, solid = all_phi[q], all_stress[q], all_solid[q]
+            flow = 0.1 * phi * s1[q * cap : (q + 1) * cap] * stress
+            base = g * part + q * cap
+            for l0 in range(0, cap, 8):
+                l1 = min(l0 + 8, cap)
+                at = pl.ds(base + l0, l1 - l0)
+                old = old_state[at]
+                decay = jnp.exp(phi[l0:l1][:, None, :] * speed[None])
+                new = decay * old + 0.15 * (1.0 - decay) * stress[l0:l1][:, None, :]
+                new_state[at] = new
+                kelvin = jnp.sum(new - old, axis=1)
+                change[o, l0:l1, :] = solid[l0:l1] * kelvin + flow[l0:l1]
+            pl.when(o != me)(lambda o=o: row_copy(o, me).start())
+        write(g).start()
+        return carry
+
+    lax.fori_loop(0, n_gz, group, 0)
+    back[me] = change[me]
 
     def finish(i, carry):
         o = partner(i, n, me)
@@ -561,14 +537,23 @@
     lax.fori_loop(0, n - 1, finish, 0)
     per_row = cols // SITES
 
-    def place(g, carry):
+    def place_cells(g, carry):
         r = pl.multiple_of(g * 8, 8)
         for j in range(per_row):
-            lines = [back[pl.ds(where[(r + k) * per_row + j], 1), :] for k in range(8)]
+            lines = []
+            for k in range(8):
+                w = where[(r + k) * per_row + j]
+                lines.append(back[w // 256, pl.ds(lax.rem(w, 256), 1), :])
             out[pl.ds(r, 8), j * SITES : (j + 1) * SITES] = jnp.concatenate(lines, axis=0)
         return carry
 
-    lax.fori_loop(0, rows // 8, place, 0)
+    lax.fori_loop(0, rows // 8, place_cells, 0)
+
+    def end(i, carry):
+        write(turn(i)).wait()
+        return carry
+
+    lax.fori_loop(0, n_gz, end, 0)
 
 
 def send_back(n_gz, n_gy, change, where, out, back, out_sems, in_sems):
@@ -642,7 +627,7 @@
     held = (block % per_row) * rows + block // per_row
     solid_slot = jnp.sum(jnp.where(hit, jnp.repeat(solid, per_row)[None, :], 0.0), axis=1)
     solid_rows = jnp.pad(solid_slot.reshape(n, cap), ((0, 0), (0, SITES - cap)))
-    lean = cap >= DIRECT + 8 and n % 8 == 0 and n_gy == 4
+    lean = cap >= DIRECT + 8 and n % 8 == 0 and n_gy == 4 and GROUP * cap % 8 == 0
     owner = flat // cap
     earlier = flat[None, :] < flat[:, None]
     if lean:
@@ -659,7 +644,6 @@
         index, spill_index = index[: n * DIRECT], index[n * DIRECT :]
         slot_map = jnp.pad(slot_map.reshape(n, cap).astype(f32), ((0, 0), (0, SITES - cap)))
         count = jnp.broadcast_to(spilled.astype(f32), (n, SITES))
-        where_back = jnp.minimum(target, n * DIRECT + SPILL - 1)
         notes = [slot_map, solid_rows, count]
     else:
         index = spill_index = jnp.zeros((8,), jnp.int32)
@@ -761,52 +745,27 @@
         return cells, chain_after, micro_after
 
     def lean_tail(got, got_spill):
-        depth = n // 8
-        whole = pl.BlockSpec((n, SPILL, SITES), lambda i: (0, 0, 0))
-        chain_after, micro_after, change, change_spill = pl.pallas_call(
-            functools.partial(creep_lean, cap, depth),
-            grid=(n // GROUP,),
-            out_shape=state_shapes
-            + (
-                jax.ShapeDtypeStruct((n, DIRECT, SITES), f32),
-                jax.ShapeDtypeStruct((n, SPILL, SITES), f32),
-            ),
-            in_specs=[
-                pl.BlockSpec((GROUP, 2 * DIRECT, SITES), lambda i: (i, 0, 0)),
-                pl.BlockSpec((n, 2 * SPILL, SITES), lambda i: (0, 0, 0)),
-                pl.BlockSpec((GROUP, 8, SITES), lambda i: (i, 0, 0)),
-                *state_specs,
-            ],
-            out_specs=(
-                *state_specs,
-                pl.BlockSpec((GROUP, DIRECT, SITES), lambda i: (i, 0, 0)),
-                whole,
-            ),
-            compiler_params=pltpu.CompilerParams(vmem_limit_bytes=limit),
-            name="creep_lean",
-        )(got, got_spill, notes_in, chain, micro)
-        cells = pl.pallas_call(
-            functools.partial(send_back_lean, n_gz, n_gy),
-            out_shape=field,
-            in_specs=[vm, vm, sm],
-            out_specs=vm,
+        where = owner * 256 + flat % cap
+        cells, micro_after, chain_after = pl.pallas_call(
+            functools.partial(creep_and_return, n_gz, n_gy, cap),
+            out_shape=(field, state_shapes[1], state_shapes[0]),
+            in_specs=[vm, vm, vm, vm, sm, hbm],
+            out_specs=(vm, vm, hbm),
             scratch_shapes=[
-                pltpu.VMEM((n * DIRECT + SPILL, SITES), f32),
-                pltpu.VMEM((7 * depth, SPILL, SITES), f32),
-                pltpu.VMEM((4 * depth, SPILL, SITES), f32),
-                pltpu.VMEM((2 * depth, SPILL, SITES), f32),
-                pltpu.VMEM((depth, SPILL, SITES), f32),
-                pltpu.VMEM((depth, SPILL, SITES), f32),
+                pltpu.VMEM(chain.shape, f32),
+                pltpu.VMEM(chain.shape, f32),
+                pltpu.VMEM((n, cap, SITES), f32),
+                pltpu.VMEM((n, cap, SITES), f32),
+                pltpu.SemaphoreType.DMA((n_gz,)),
+                pltpu.SemaphoreType.DMA((n_gz,)),
                 pltpu.SemaphoreType.DMA((n,)),
                 pltpu.SemaphoreType.DMA((n,)),
-                pltpu.SemaphoreType.DMA((depth + 3,)),
-                pltpu.SemaphoreType.DMA((depth + 3,)),
             ],
             compiler_params=pltpu.CompilerParams(
                 collective_id=3, has_side_effects=True, vmem_limit_bytes=limit
             ),
-            name="send_back_lean",
-        )(change, change_spill, where_back)
+            name="creep_and_return",
+        )(got, got_spill, notes_in, micro, where, chain)
         return cells, chain_after, micro_after
 
     if lean:

time: 103 us -> 102 us (level)
  Pallas kernels: 89.6 us -> 81.8 us
  local copies, waits for them, and re-layouts: 5.25 us -> 12 us
    pallas_call x2 -> x1, Pallas kernels: 43.6 us -> 36.2 us  [lean_tail(): pl.pallas_call(functools.partial(creep_and_return, n_gz, n_gy, cap), out_...]
    unnamed x12 -> x14, local copies, waits for them, and re-layouts: 4.43 us -> 11.2 us
where the time goes in v3:
time: 102 us
  Pallas kernels  81.8 us (80%)
  local copies, waits for them, and re-layouts  12 us (12%)
  other arithmetic  6.08 us (6%)
  between operations  2.12 us (2%)
    pallas_call x1, Pallas kernels, body(): pl.pallas_call(functools.partial(sweep_and_send, n_gz, n_gy, lean), out_s...  45.6 us
    pallas_call x1, Pallas kernels, lean_tail(): pl.pallas_call(functools.partial(creep_and_return, n_gz, n_gy, cap), out_...  36.2 us
    unnamed x14, local copies, waits for them, and re-layouts  11.2 us

profile of v3, /device:TPU:0, one launch (start us, length us, event | category | flops | bytes accessed | tf_op | source)
XLA Modules:
  0.0 102.0 jit_solution(12200062101189880353)
XLA Ops:
  0.6 0.7 sqrt_add_fusion
  1.7 0.8 copy.18.tally
  2.5 0.8 copy.17
  3.4 0.6 select_reduce_fusion.1
  4.0 0.4 convert_reduce_fusion.1
  4.4 0.6 convert_reduce_fusion.2
  5.7 0.4 convert_reduce_fusion
  6.1 0.6 select_reduce_fusion.2
  6.7 0.3 select_reduce_fusion.3
  7.3 0.1 stack.15.notes
  7.4 0.9 iota_compare_fusion
  8.3 1.0 copy-done
  9.3 1.0 copy-done.1
  10.2 1.0 copy-done.2
  11.2 45.6 %sweep_and_send.1 = (f32[48,1536]{1,0:T(8,128)S(1)}, f32[48,1536]{1,0:T(8,128)S(1)}, f32[48,1536]{1,0:T(8,128)S(1)}, f32[2,584,128]{2,1,0:T(8,128)}, f32[32,8,12...) custom-call(f32[48,1536]{1,0:T(8,128)S(1)} %copy-done, f32[48,1536]{1,0:T(8,128)S(1)} %copy-done.1, ...), custom_call_target="tpu_custom_call" | custom-call | tf_op jit(solution)/shard_map/sweep_and_send/pallas_call | solution.py:680
  56.8 1.5 %slice_reduce_fusion = f32[]{:T(128)} fusion(f32[32,8,128]{2,1,0:T(8,128)} %get-tuple-element.159), kind=kLoop, calls=%fused_computation.33 | loop fusion | flops 31 | bytes 132 | tf_op jit(solution)/shard_map/reduce_max | solution.py:772
  59.0 36.3 %conditional.1 = (f32[48,1536]{1,0:T(8,128)S(1)}, f32[1728,8,128]{2,1,0:T(8,128)S(1)}, f32[1728,128]{1,0:T(8,128)S(1)}) conditional(s32[]{:T(128)} %convert_element_type.36, (s32[576]{0:T(1024)S(1)}, s32[576]{0:T(1024)S(1)}, pred[576]{0:T(1024)(128)(4,1)S(1)}, s32[576]{0:T(1024)S(1)}, s32[576]{0:T(1024)S(1)}, /*index=5*/s32[576]{0:T(1024)S(1)}, ...), branch_computations={%region_7.9_spmd, %region_9.10_spmd} | conditional | flops 2005632 | bytes 1042008 | solution.py:773
  59.0 36.2 %creep_and_return.1 = (f32[48,1536]{1,0:T(8,128)S(1)}, f32[1728,128]{1,0:T(8,128)S(1)}, f32[1728,8,128]{2,1,0:T(8,128)S(1)}) custom-call(f32[32,48,128]{2,1,0:T(8,128)} %get-tuple-element.127.got, f32[32,80,128]{2,1,0:T(8,128)S(1)} %get-tuple-element.128.spill, f32[32,8,128]{2,1,0:T(8,128)} %get-tuple-element.129.notes, ...), custom_call_target="tpu_custom_call" | custom-call | tf_op jit(solution)/shard_map/cond/branch_1_fun/creep_and_return/pallas_call | solution.py:749
  95.3 0.7 copy.31
  96.0 0.7 copy.32
  96.7 0.7 copy.33
  97.4 0.7 copy.34
  98.1 3.0 %copy.35 = f32[1728,8,128]{2,1,0:T(8,128)} copy(f32[1728,8,128]{2,1,0:T(8,128)S(1)} %get-tuple-element.192) | data formatting | bytes 14155776
  101.1 0.9 copy.36
  (28 shorter events, 0.8 us)
Async XLA Ops:
  8.3 1.0 copy-start
  9.3 1.0 copy-start.1
  10.2 1.0 copy-start.2

commit v4 on v3

--- a/solution.py
+++ b/solution.py
@@ -15,8 +15,8 @@
 PAD = 128
 TOP = 8
 GROUP = 4
-DIRECT = 24
-SPILL = 40
+DIRECT = 32
+SPILL = 24
 DRY = 0.05 + 0.95 / (1.0 + 5.0**16)
 MESH = pl.DeviceIdType.MESH
 
@@ -60,22 +60,33 @@
 
 def sweep_and_send(
     n_gz, n_gy, lean,
-    warmth, moisture, degree, tally, index, spill_index, notes,
+    warmth_hbm, moisture_hbm, degree_hbm, tally_hbm, index, spill_index, notes,
     temp_out, hum_out, degree_out, blocks, notes_in, *rest,
 ):
     if lean:
         got, got_spill = rest[:2]
         rest = rest[2:]
     ext, diff, z_send, z_recv, z_sems, y_sems, note_out, note_in = rest[:8]
+    degree, tally, load_sems = rest[8:11]
     if lean:
-        send, out_sems, in_sems, own_sems, relay_out, relay_in = rest[8:]
+        send, out_sems, in_sems, own_sems, relay_out, relay_in = rest[11:]
     n = n_gz * n_gy
-    rows, cols = warmth.shape
+    rows, cols = degree.shape
     wide = cols + 2 * PAD
     per_row = cols // SITES
     gz = lax.axis_index("gz")
     gy = lax.axis_index("gy")
     me = gz * n_gy + gy
+    inner = slice(PAD, PAD + cols)
+    body_rows = slice(TOP, TOP + rows)
+    loads = [
+        pltpu.make_async_copy(warmth_hbm, ext.at[0, 0, body_rows, inner], load_sems.at[0]),
+        pltpu.make_async_copy(moisture_hbm, ext.at[0, 1, body_rows, inner], load_sems.at[1]),
+        pltpu.make_async_copy(degree_hbm, degree, load_sems.at[2]),
+        pltpu.make_async_copy(tally_hbm, tally, load_sems.at[3]),
+    ]
+    for load in loads:
+        load.start()
     greet_all(n, n_gy, me)
 
     def note_copy(o, at):
@@ -95,11 +106,8 @@
     x = lax.rem(lax.broadcasted_iota(jnp.int32, (8, cols), 1), NX)
     has_west = x > 0
     has_east = x < NX - 1
-    inner = slice(PAD, PAD + cols)
-    body_rows = slice(TOP, TOP + rows)
-
-    ext[0, 0, body_rows, inner] = warmth[...]
-    ext[0, 1, body_rows, inner] = moisture[...]
+    for load in loads:
+        load.wait()
 
     for s in range(SWEEPS):
         for f in range(2):
@@ -205,8 +213,8 @@
                 c = 0.5 * (d0 + dg)
                 conduct = c if conduct is None else conduct + c
                 inflow = c * g if inflow is None else inflow + c * g
-            t1 = (warmth[own, :] + 4.0 * progress + total) / 7.0
-            h1 = (moisture[own, :] - 0.5 * progress + inflow) / (1.0 + conduct)
+            t1 = (ext[0, 0, here, inner] + 4.0 * progress + total) / 7.0
+            h1 = (ext[0, 1, here, inner] - 0.5 * progress + inflow) / (1.0 + conduct)
             if s < SWEEPS - 1:
                 ext[s + 1, 0, here, inner] = t1
                 ext[s + 1, 1, here, inner] = h1
@@ -444,7 +452,8 @@
         return pltpu.make_async_copy(new_state.at[at], chain_out.at[at], write_sems.at[g])
 
     def turn(i):
-        return lax.rem(gz + n_gz // 2 + i, n_gz)
+        mid = n_gz // 2
+        return lax.rem(gz // mid + 1 + i // mid, 2) * mid + lax.rem(gz + i, mid)
 
     def begin(i, carry):
         read(turn(i)).start()
@@ -615,6 +624,7 @@
     vm = pl.BlockSpec(memory_space=pltpu.VMEM)
     sm = pl.BlockSpec(memory_space=pltpu.SMEM)
     hbm = pl.BlockSpec(memory_space=pl.ANY)
+    far = pl.BlockSpec(memory_space=pltpu.HBM)
     f32 = jnp.float32
 
     local_times = lax.dynamic_slice_in_dim(pouring, lax.axis_index("gz") * lifts, lifts)
@@ -662,6 +672,9 @@
         pltpu.SemaphoreType.DMA((SWEEPS, 2, 2)),
         pltpu.SemaphoreType.DMA((n,)),
         pltpu.SemaphoreType.DMA((n,)),
+        pltpu.VMEM((rows, cols), f32),
+        pltpu.VMEM((rows, per_row), jnp.int32),
+        pltpu.SemaphoreType.DMA((4,)),
     ]
     out_specs = [vm] * 5
     if lean:
@@ -680,11 +693,11 @@
     results = pl.pallas_call(
         functools.partial(sweep_and_send, n_gz, n_gy, lean),
         out_shape=tuple(outs),
-        in_specs=[vm, vm, vm, vm, sm, sm, vm],
+        in_specs=[far, far, far, far, sm, sm, vm],
         out_specs=tuple(out_specs),
         scratch_shapes=scratch,
         compiler_params=pltpu.CompilerParams(
-            collective_id=0, has_side_effects=True, vmem_limit_bytes=limit
+            collective_id=0, has_side_effects=True, vmem_limit_bytes=60 * 1024 * 1024
         ),
         name="sweep_and_send",
     )(warmth, moisture, degree, tally, index, spill_index, notes)
@@ -700,7 +713,8 @@
     )
 
     def dense_tail(*_):
-        index = nb + jnp.sum(jnp.where(hit, held[None, :] - nb, 0), axis=1)
+        held_there = flat[None, :] == slot_id[:, None]
+        index = nb + jnp.sum(jnp.where(held_there, held[None, :] - nb, 0), axis=1)
         where = (flat // cap) * cp + flat % cap
         got = pl.pallas_call(
             functools.partial(send_dense, n_gz, n_gy, cap),

time: 102 us -> 102 us (level)
  other arithmetic: 6.08 us -> 4.34 us
  local copies, waits for them, and re-layouts: 12 us -> 13.4 us
    pallas_call x1, Pallas kernels: 36.2 us -> 31.4 us  [lean_tail(): pl.pallas_call(functools.partial(creep_and_return, n_gz, n_gy, cap), out_...]
    pallas_call x1, Pallas kernels: 45.6 us -> 50.1 us  [body(): pl.pallas_call(functools.partial(sweep_and_send, n_gz, n_gy, lean), out_s...]
    slice x1 -> x2, local copies, waits for them, and re-layouts: 0.01 us -> 1.11 us  [body(): index, spill_index = (index[:n * DIRECT], index[n * DIRECT:])]
    unnamed x14 -> x10, local copies, waits for them, and re-layouts: 11.2 us -> 10.9 us
where the time goes in v4:
time: 102 us; the launch traced here: 101 us
  Pallas kernels  81.5 us (80%)
  local copies, waits for them, and re-layouts  13.4 us (13%)
  other arithmetic  4.34 us (4%)
  between operations  2.12 us (2%)
    pallas_call x1, Pallas kernels, body(): pl.pallas_call(functools.partial(sweep_and_send, n_gz, n_gy, lean), out_s...  50.1 us
    pallas_call x1, Pallas kernels, lean_tail(): pl.pallas_call(functools.partial(creep_and_return, n_gz, n_gy, cap), out_...  31.4 us
    unnamed x10, local copies, waits for them, and re-layouts  10.9 us

profile of v4, /device:TPU:0, one launch (start us, length us, event | category | flops | bytes accessed | tf_op | source)
XLA Modules:
  0.0 101.4 jit_solution(5239812872027993548)
XLA Ops:
  0.6 0.7 sqrt_add_fusion
  1.6 0.1 broadcast_in_dim.68
  1.7 1.4 %copy.19.tally_hbm = s32[48,12]{1,0:T(8,128)} copy(s32[48,12]{0,1:T(8,128)} %param.13) | data formatting | bytes 4608 | tf_op args[3]
  3.1 0.8 copy.18
  4.0 0.6 select_reduce_fusion.1
  4.6 0.4 convert_reduce_fusion.1
  5.1 0.6 convert_reduce_fusion.2
  6.3 0.4 convert_reduce_fusion
  6.7 0.5 select_reduce_fusion.2
  7.3 0.1 convert_element_type.32
  7.4 0.3 select_reduce_fusion.3
  7.8 0.5 slice.13.spill_index
  8.3 0.6 slice.12.index
  9.0 0.8 stack.15.notes
  9.8 50.1 %sweep_and_send.1 = (f32[48,1536]{1,0:T(8,128)}, f32[48,1536]{1,0:T(8,128)}, f32[48,1536]{1,0:T(8,128)}, f32[2,584,128]{2,1,0:T(8,128)S(1)}, f32[32,8,128]{2,1,0...) custom-call(f32[48,1536]{1,0:T(8,128)} %warmth_hbm.1, f32[48,1536]{1,0:T(8,128)} %moisture_hbm.1, ...), custom_call_target="tpu_custom_call" | custom-call | tf_op jit(solution)/shard_map/sweep_and_send/pallas_call | solution.py:693
  59.9 0.6 slice_reduce_fusion
  61.3 31.5 %conditional.1 = (f32[48,1536]{1,0:T(8,128)S(1)}, f32[1728,8,128]{2,1,0:T(8,128)S(1)}, f32[1728,128]{1,0:T(8,128)S(1)}) conditional(s32[]{:T(128)} %convert_element_type.36, (s32[48,12]{0,1:T(8,128)}, s32[1728]{0:T(1024)S(1)}, s32[576]{0:T(1024)S(1)}, f32[2,584,128]{2,1,0:T(8,128)S(1)}, f32[32,128]{1,0:T(8,128)S(1)}, ...), branch_computations={%region_7.9_spmd, %region_9.10_spmd} | conditional | flops 2994624 | bytes 50712 | solution.py:787
  61.3 31.4 %creep_and_return.1 = (f32[48,1536]{1,0:T(8,128)S(1)}, f32[1728,128]{1,0:T(8,128)S(1)}, f32[1728,8,128]{2,1,0:T(8,128)S(1)}) custom-call(f32[32,64,128]{2,1,0:T(8,128)S(1)} %get-tuple-element.59.got, f32[32,48,128]{2,1,0:T(8,128)S(1)} %get-tuple-element.60.spill, f32[32,8,128]{2,1,0:T(8,128)S(1)} %get-tuple-element.61.notes, ...), custom_call_target="tpu_custom_call" | custom-call | tf_op jit(solution)/shard_map/cond/branch_1_fun/creep_and_return/pallas_call | solution.py:763
  92.7 1.7 %copy.33 = f32[48,1536]{1,0:T(8,128)} copy(f32[48,1536]{1,0:T(8,128)} %get-tuple-element.134) | data formatting | bytes 589824
  94.4 1.7 %copy.34 = f32[48,1536]{1,0:T(8,128)} copy(f32[48,1536]{1,0:T(8,128)} %get-tuple-element.135) | data formatting | bytes 589824
  96.1 0.7 copy.35
  96.8 0.7 copy.36
  97.6 3.0 %copy.37 = f32[1728,8,128]{2,1,0:T(8,128)} copy(f32[1728,8,128]{2,1,0:T(8,128)S(1)} %get-tuple-element.138) | data formatting | bytes 14155776
  100.5 0.9 copy.38
  (22 shorter events, 0.6 us)
Async XLA Ops:
  61.3 34.9 %copy-start = (f32[48,1536]{1,0:T(8,128)S(1)}, f32[48,1536]{1,0:T(8,128)}, u32[]{:S(2)}) copy-start(f32[48,1536]{1,0:T(8,128)} %get-tuple-element.136) | copy-start | bytes 884740

commit v5 on v4

--- a/solution.py
+++ b/solution.py
@@ -15,8 +15,8 @@
 PAD = 128
 TOP = 8
 GROUP = 4
-DIRECT = 32
-SPILL = 24
+DIRECT = 24
+SPILL = 40
 DRY = 0.05 + 0.95 / (1.0 + 5.0**16)
 MESH = pl.DeviceIdType.MESH
 
@@ -60,7 +60,7 @@
 
 def sweep_and_send(
     n_gz, n_gy, lean,
-    warmth_hbm, moisture_hbm, degree_hbm, tally_hbm, index, spill_index, notes,
+    warmth_hbm, moisture_hbm, degree_hbm, tally_hbm, index, notes,
     temp_out, hum_out, degree_out, blocks, notes_in, *rest,
 ):
     if lean:
@@ -255,7 +255,7 @@
 
         line = (core * 4 + x * 2 + y) * depth
         for l in range(SPILL):
-            k = spill_index[l]
+            k = index[n * DIRECT + l]
             got_spill[line + z, l : l + 1, :] = blocks[0, pl.ds(k, 1), :]
             got_spill[line + z, SPILL + l : SPILL + l + 1, :] = blocks[1, pl.ds(k, 1), :]
 
@@ -551,7 +551,7 @@
         for j in range(per_row):
             lines = []
             for k in range(8):
-                w = where[(r + k) * per_row + j]
+                w = where[j * rows + r + k]
                 lines.append(back[w // 256, pl.ds(lax.rem(w, 256), 1), :])
             out[pl.ds(r, 8), j * SITES : (j + 1) * SITES] = jnp.concatenate(lines, axis=0)
         return carry
@@ -605,7 +605,7 @@
     def place(g, carry):
         r = pl.multiple_of(g * 8, 8)
         for j in range(per_row):
-            lines = [back[pl.ds(where[(r + k) * per_row + j], 1), :] for k in range(8)]
+            lines = [back[pl.ds(where[j * rows + r + k], 1), :] for k in range(8)]
             out[pl.ds(r, 8), j * SITES : (j + 1) * SITES] = jnp.concatenate(lines, axis=0)
         return carry
 
@@ -630,12 +630,11 @@
     local_times = lax.dynamic_slice_in_dim(pouring, lax.axis_index("gz") * lifts, lifts)
     age = 2400.0 - jnp.repeat(local_times, LIFT).astype(f32)
     solid = jnp.sqrt(600.0 / age) + 0.2
-    flat = keeper.reshape(-1)
+    flat = keeper.T.reshape(-1)
     slot_id = jnp.arange(slots, dtype=jnp.int32)
     hit = flat[None, :] == slot_id[:, None]
     block = jnp.arange(nb, dtype=jnp.int32)
-    held = (block % per_row) * rows + block // per_row
-    solid_slot = jnp.sum(jnp.where(hit, jnp.repeat(solid, per_row)[None, :], 0.0), axis=1)
+    solid_slot = jnp.sum(jnp.where(hit, jnp.tile(solid, per_row)[None, :], 0.0), axis=1)
     solid_rows = jnp.pad(solid_slot.reshape(n, cap), ((0, 0), (0, SITES - cap)))
     lean = cap >= DIRECT + 8 and n % 8 == 0 and n_gy == 4 and GROUP * cap % 8 == 0
     owner = flat // cap
@@ -650,13 +649,12 @@
         target = jnp.where(over, n * DIRECT + spot, owner * DIRECT + rank)
         line_id = jnp.arange(n * DIRECT + SPILL, dtype=jnp.int32)
         fits = target[None, :] == line_id[:, None]
-        index = nb + jnp.sum(jnp.where(fits, held[None, :] - nb, 0), axis=1)
-        index, spill_index = index[: n * DIRECT], index[n * DIRECT :]
+        index = nb + jnp.sum(jnp.where(fits, block[None, :] - nb, 0), axis=1)
         slot_map = jnp.pad(slot_map.reshape(n, cap).astype(f32), ((0, 0), (0, SITES - cap)))
         count = jnp.broadcast_to(spilled.astype(f32), (n, SITES))
         notes = [slot_map, solid_rows, count]
     else:
-        index = spill_index = jnp.zeros((8,), jnp.int32)
+        index = jnp.zeros((8,), jnp.int32)
         notes = [solid_rows, solid_rows, solid_rows]
     notes = jnp.stack(notes + [jnp.zeros((n, SITES), f32)] * 5, axis=1)
 
@@ -693,14 +691,14 @@
     results = pl.pallas_call(
         functools.partial(sweep_and_send, n_gz, n_gy, lean),
         out_shape=tuple(outs),
-        in_specs=[far, far, far, far, sm, sm, vm],
+        in_specs=[far, far, far, far, sm, vm],
         out_specs=tuple(out_specs),
         scratch_shapes=scratch,
         compiler_params=pltpu.CompilerParams(
             collective_id=0, has_side_effects=True, vmem_limit_bytes=60 * 1024 * 1024
         ),
         name="sweep_and_send",
-    )(warmth, moisture, degree, tally, index, spill_index, notes)
+    )(warmth, moisture, degree, tally, index, notes)
     temp, hum, degree_after, blocks, notes_in = results[:5]
 
     state_specs = (
@@ -714,7 +712,7 @@
 
     def dense_tail(*_):
         held_there = flat[None, :] == slot_id[:, None]
-        index = nb + jnp.sum(jnp.where(held_there, held[None, :] - nb, 0), axis=1)
+        index = nb + jnp.sum(jnp.where(held_there, block[None, :] - nb, 0), axis=1)
         where = (flat // cap) * cp + flat % cap
         got = pl.pallas_call(
             functools.partial(send_dense, n_gz, n_gy, cap),

time: 102 us -> 103 us (level)
    pallas_call x1, Pallas kernels: 31.4 us -> 36.5 us  [lean_tail(): pl.pallas_call(functools.partial(creep_and_return, n_gz, n_gy, cap), out_...]
    pallas_call x1, Pallas kernels: 50.1 us -> 45.9 us  [body(): pl.pallas_call(functools.partial(sweep_and_send, n_gz, n_gy, lean), out_s...]
    slice x2 -> x0, local copies, waits for them, and re-layouts: 1.11 us -> none  [body(): index, spill_index = (index[:n * DIRECT], index[n * DIRECT:])]
    unnamed x10 -> x7, local copies, waits for them, and re-layouts: 10.9 us -> 11.1 us
where the time goes in v5:
time: 103 us
  Pallas kernels  82.4 us (80%)
  local copies, waits for them, and re-layouts  13.1 us (13%)
  other arithmetic  4.98 us (5%)
  between operations  2.07 us (2%)
    pallas_call x1, Pallas kernels, body(): pl.pallas_call(functools.partial(sweep_and_send, n_gz, n_gy, lean), out_s...  45.9 us
    pallas_call x1, Pallas kernels, lean_tail(): pl.pallas_call(functools.partial(creep_and_return, n_gz, n_gy, cap), out_...  36.5 us
    unnamed x7, local copies, waits for them, and re-layouts  11.1 us

profile of v5, /device:TPU:0, one launch (start us, length us, event | category | flops | bytes accessed | tf_op | source)
XLA Modules:
  0.0 102.5 jit_solution(13983540475125342525)
XLA Ops:
  0.6 0.7 sqrt_add_fusion
  1.5 0.8 lt.28
  2.3 0.4 convert_reduce_fusion.1
  2.8 0.6 convert_reduce_fusion.2
  4.0 0.4 convert_reduce_fusion
  4.4 0.5 select_reduce_fusion.2
  5.0 0.3 select_reduce_fusion.3
  5.3 0.6 broadcast_add_fusion.2.index
  6.0 0.6 select_reduce_fusion.1
  6.6 0.1 reshape.111
  6.7 0.1 convert_element_type.36
  6.8 1.4 %copy.15.tally_hbm = s32[48,12]{1,0:T(8,128)} copy(s32[48,12]{0,1:T(8,128)} %param.13) | data formatting | bytes 4608 | tf_op args[3]
  8.2 0.8 stack.15.notes
  9.0 45.9 %sweep_and_send.1 = (f32[48,1536]{1,0:T(8,128)}, f32[48,1536]{1,0:T(8,128)}, f32[48,1536]{1,0:T(8,128)}, f32[2,584,128]{2,1,0:T(8,128)S(1)}, f32[32,8,128]{2,1,0...) custom-call(f32[48,1536]{1,0:T(8,128)} %warmth_hbm.1, f32[48,1536]{1,0:T(8,128)} %moisture_hbm.1, ...), custom_call_target="tpu_custom_call" | custom-call | tf_op jit(solution)/shard_map/sweep_and_send/pallas_call | solution.py:691
  54.9 0.6 slice_reduce_fusion
  56.2 36.7 %conditional.1 = (f32[48,1536]{1,0:T(8,128)S(1)}, f32[1728,8,128]{2,1,0:T(8,128)S(1)}, f32[1728,128]{1,0:T(8,128)S(1)}) conditional(s32[]{:T(128)} %convert_element_type.40, (s32[12,48]{1,0:T(8,128)}, s32[1728]{0:T(1024)S(1)}, s32[576]{0:T(1024)S(1)}, f32[2,584,128]{2,1,0:T(8,128)S(1)}, f32[32,128]{1,0:T(8,128)S(1)}, ...), branch_computations={%region_7.9_spmd, %region_9.10_spmd} | conditional | flops 2994624 | bytes 46104 | solution.py:785
  56.2 0.1 fusion.4.where
  56.3 36.5 %creep_and_return.1 = (f32[48,1536]{1,0:T(8,128)S(1)}, f32[1728,128]{1,0:T(8,128)S(1)}, f32[1728,8,128]{2,1,0:T(8,128)S(1)}) custom-call(f32[32,48,128]{2,1,0:T(8,128)S(1)} %get-tuple-element.59.got, f32[32,80,128]{2,1,0:T(8,128)S(1)} %get-tuple-element.60.spill, f32[32,8,128]{2,1,0:T(8,128)S(1)} %get-tuple-element.61.notes, ...), custom_call_target="tpu_custom_call" | custom-call | tf_op jit(solution)/shard_map/cond/branch_1_fun/creep_and_return/pallas_call | solution.py:761
  92.9 1.7 %copy.28 = f32[48,1536]{1,0:T(8,128)} copy(f32[48,1536]{1,0:T(8,128)} %get-tuple-element.116) | data formatting | bytes 589824
  94.6 1.7 %copy.29 = f32[48,1536]{1,0:T(8,128)} copy(f32[48,1536]{1,0:T(8,128)} %get-tuple-element.117) | data formatting | bytes 589824
  96.2 1.7 %copy.30 = f32[48,1536]{1,0:T(8,128)} copy(f32[48,1536]{1,0:T(8,128)} %get-tuple-element.118) | data formatting | bytes 589824
  97.9 0.7 copy.31
  98.7 3.0 %copy.32 = f32[1728,8,128]{2,1,0:T(8,128)} copy(f32[1728,8,128]{2,1,0:T(8,128)S(1)} %get-tuple-element.120) | data formatting | bytes 14155776
  101.6 0.9 copy.33
  (15 shorter events, 0.3 us)
